TPU v7x, 128 devices: a whole 4x4x4 slice. The times are simulated.
128 devices in a mesh: row: 4 (over x_hi, core), col: 32 (over z, y, x_lo).
Axes of the slice: x: 4 (x_hi: 2, x_lo: 2; x = x_hi * 2 + x_lo), y: 4, z: 4, core: 2. Of those that a mesh axis runs over, the one named last changes fastest.
Arguments:
- scalar_field: bfloat16 [768, 768, 1024], P('row', 'col'), may hold values from -6 to 6
- x_operator: bfloat16 [1024, 1024], replicated, may hold values from -0.1875 to 0.1875
- y_second: bfloat16 [768, 768], replicated, may hold values from -0.21875 to 0.21875
- y_first: bfloat16 [768, 768], replicated, may hold values from -0.21875 to 0.21875
- y_stretch: float32 [768], replicated, may hold values from 0.5 to 2
- y_curve: float32 [768], replicated, may hold values from -3 to 3
- z_operator: bfloat16 [768, 768], replicated, may hold values from -0.21875 to 0.21875
Outputs:
- diffusion: bfloat16 [768, 768, 1024], P('row', 'col')
All inputs are finite; a program needn't handle non-finite values.
Results may differ from a plain program's by a relative error of at most 0.0052.
Values may be sent and summed in bfloat16 or wider, within the bound.
A program may use at most 192 MiB of HBM per device.

v0:
```python
import jax
import jax.numpy as jnp
from jax import lax
from jax.sharding import PartitionSpec as P


def x_apply(scalar_field, x_operator):
    flat = scalar_field.reshape(-1, scalar_field.shape[2])
    product = jnp.dot(flat, x_operator, preferred_element_type=jnp.float32)
    return product.reshape(scalar_field.shape[0], scalar_field.shape[1], x_operator.shape[1])


def per_device(scalar_field, x_operator, y_second, y_first, y_stretch, y_curve, z_operator):
    y_combined = (
        y_stretch[None, :] * y_second.astype(jnp.float32)
        + y_curve[None, :] * y_first.astype(jnp.float32)
    ).astype(jnp.bfloat16)
    x_term = x_apply(scalar_field, x_operator)
    columns = lax.all_to_all(scalar_field, "row", split_axis=2, concat_axis=0, tiled=True)
    y_term = jnp.einsum("yzx,yk->kzx", columns, y_combined, preferred_element_type=jnp.float32)
    pencil_y, y_term = (columns, y_term.astype(jnp.bfloat16))
    pencil_z = lax.all_to_all(pencil_y, "col", split_axis=0, concat_axis=1, tiled=True)
    z_full = jnp.einsum("yzx,zk->ykx", pencil_z, z_operator, preferred_element_type=jnp.float32)
    z_in_y = lax.all_to_all(
        z_full.astype(jnp.bfloat16), "col", split_axis=1, concat_axis=0, tiled=True
    )
    y_back, z_back = (
        lax.all_to_all(y_term, "row", split_axis=0, concat_axis=2, tiled=True),
        lax.all_to_all(z_in_y, "row", split_axis=0, concat_axis=2, tiled=True),
    )
    total = x_term + y_back.astype(jnp.float32) + z_back.astype(jnp.float32)
    return total.astype(jnp.bfloat16)


def solution(mesh):
    in_specs = (P("row", "col", None), P(), P(), P(), P(), P(), P())
    out_specs = P("row", "col", None)
    return jax.shard_map(
        per_device, mesh=mesh, in_specs=in_specs, out_specs=out_specs, check_vma=False
    )
```

profile of v0, /device:TPU:0, one launch (start us, length us, event | category | flops | bytes accessed | tf_op | source)
XLA Modules:
  0.0 749.5 jit_solution(9884640975297752104)
XLA Ops:
  0.0 0.0 copy-start
  0.0 17.7 %copy.42 = bf16[192,24,1024]{0,1,2:T(8,128)(2,1)} copy(bf16[192,24,1024]{2,1,0:T(8,128)(2,1)} %param.7) | data formatting | bytes 18874368 | tf_op args[0]
  17.7 148.9 %all_to_all.72 = bf16[192,24,1024]{0,1,2:T(8,128)(2,1)} all-to-all(bf16[192,24,1024]{0,1,2:T(8,128)(2,1)} %copy.42), channel_id=1, replica_groups=mesh['row'=4,'col'=32] {'row'}, dimensions={2} | all-to-all | bytes 18874368 | tf_op jit(solution)/shard_map/all_to_all | solution.py:19
  166.6 17.4 %copy.58 = bf16[192,24,4,256]{3,1,0,2:T(8,128)(2,1)} copy(bf16[192,24,4,256]{0,1,3,2:T(8,128)(2,1)} %bitcast.38) | data formatting | bytes 18874368 | tf_op jit(solution)/shard_map/all_to_all | solution.py:19
  184.0 116.8 %all_to_all.73 = bf16[768,24,256]{2,1,0:T(8,128)(2,1)} all-to-all(bf16[768,24,256]{2,1,0:T(8,128)(2,1)} %bitcast.43), channel_id=1, replica_groups=mesh['row'=4,'col'=32] {'col'}, dimensions={0} | all-to-all | bytes 18874368 | tf_op jit(solution)/shard_map/all_to_all | solution.py:22
  300.8 0.0 copy-start.1
  300.8 8.6 %copy.48 = bf16[32,24,24,256]{3,2,0,1:T(8,128)(2,1)} copy(bf16[32,24,24,256]{3,2,1,0:T(8,128)(2,1)} %bitcast.42) | data formatting | bytes 18874368 | tf_op jit(solution)/shard_map/all_to_all | solution.py:22
  309.5 0.0 copy-done.1
  309.5 13.4 %convert_bitcast_fusion.1 = bf16[24,768,256]{2,1,0:T(8,128)(2,1)} fusion(bf16[24,768,256]{2,1,0:T(8,128)(2,1)} %bitcast.45, bf16[768,768]{1,0:T(8,128)(2,1)S(1)} %copy-done.1), kind=kOutput, calls=%fused_computation.3 | convolution fusion | flops 7252475904 | bytes 20054016 | tf_op jit(solution)/shard_map/yzx,zk->ykx/dot_general | solution.py:23
  322.8 12.8 %copy.50 = bf16[24,768,256]{2,0,1:T(8,128)(2,1)} copy(bf16[24,768,256]{2,1,0:T(8,128)(2,1)} %convert_bitcast_fusion.1) | data formatting | bytes 18874368 | tf_op jit(solution)/shard_map/convert_element_type | solution.py:25
  335.6 5.2 all-to-all-start.3
  340.8 0.0 copy-start.2
  340.8 0.0 copy-start.3
  340.8 0.0 copy-start.4
  340.8 15.9 %copy.43 = bf16[192,24,4,256]{3,0,2,1:T(8,128)(2,1)} copy(bf16[192,24,4,256]{0,1,3,2:T(8,128)(2,1)} %bitcast.39) | data formatting | bytes 18874368 | tf_op jit(solution)/shard_map/all_to_all | solution.py:19
  356.7 0.0 copy-done.2
  356.7 0.0 copy-done.3
  356.7 0.0 copy-done.4
  356.7 13.9 %convolution_convert_fusion = bf16[768,24,256]{2,0,1:T(8,128)(2,1)} fusion(bf16[768,24,256]{2,0,1:T(8,128)(2,1)} %bitcast.46, bf16[768,768]{1,0:T(8,128)(2,1)S(1)} %copy-done.2, bf16[768,768]{1,0:T(8,128)(2,1)} %param.9, f32[768]{0:T(1024)S(1)} %copy-done.3, f32[768]{0:T(1024)S(1)} %copy-done.4), kind=kOutput, calls=%fused_computation.4 | convolution fusion | flops 7256014848 | bytes 21239808 | tf_op jit(solution)/shard_map/yzx,yk->kzx/dot_general | solution.py:20
  370.7 12.7 %copy.45 = bf16[768,24,256]{2,1,0:T(8,128)(2,1)} copy(bf16[768,24,256]{2,0,1:T(8,128)(2,1)} %convolution_convert_fusion) | data formatting | bytes 18874368 | tf_op jit(solution)/shard_map/convert_element_type | solution.py:21
  383.3 84.8 %all-to-all-done.3 = bf16[24,768,256]{2,0,1:T(8,128)(2,1)} async-done(((bf16[24,768,256]{2,0,1:T(8,128)(2,1)}), bf16[24,768,256]{2,0,1:T(8,128)(2,1)}, u32[]{:S(2)}, u32[]{:S(2)}) %all-to-all-start.3) | async-done | bytes 9437216 | tf_op jit(solution)/shard_map/all_to_all | solution.py:24
  468.2 14.5 %all-to-all-start.1 = ((bf16[768,24,256]{2,1,0:T(8,128)(2,1)}), bf16[768,24,256]{2,1,0:T(8,128)(2,1)}, u32[]{:S(2)}, u32[]{:S(2)}) async-start(bf16[768,24,256]{2,1,0:T(8,128)(2,1)} %copy.45), calls=%async_computation.1 | async-start | bytes 18874368 | tf_op jit(solution)/shard_map/all_to_all | solution.py:28
  482.7 10.4 %copy.52 = bf16[32,24,24,256]{3,2,1,0:T(8,128)(2,1)} copy(bf16[32,24,24,256]{3,1,2,0:T(8,128)(2,1)} %bitcast.16) | data formatting | bytes 18874368 | tf_op jit(solution)/shard_map/all_to_all | solution.py:24
  493.1 95.5 %all-to-all-done.1 = bf16[768,24,256]{2,1,0:T(8,128)(2,1)} async-done(((bf16[768,24,256]{2,1,0:T(8,128)(2,1)}), bf16[768,24,256]{2,1,0:T(8,128)(2,1)}, u32[]{:S(2)}, u32[]{:S(2)}) %all-to-all-start.1) | async-done | bytes 9437216 | tf_op jit(solution)/shard_map/all_to_all | solution.py:28
  588.7 5.8 all-to-all-start.4
  594.5 21.6 %copy.62 = f32[4,192,24,256]{3,0,2,1:T(4,128)} copy(bf16[4,192,24,256]{3,2,1,0:T(8,128)(2,1)} %bitcast.20) | data formatting | bytes 28311552 | tf_op jit(solution)/shard_map/convert_element_type | solution.py:31
  616.1 23.2 %reshape.14 = f32[192,24,1024]{2,1,0:T(8,128)} reshape(f32[192,24,4,256]{3,2,1,0:T(4,128)} %bitcast.40) | data formatting | bytes 37748736 | tf_op jit(solution)/shard_map/convert_element_type | solution.py:31
  639.3 61.1 %all-to-all-done.4 = bf16[768,24,256]{2,1,0:T(8,128)(2,1)} async-done(((bf16[768,24,256]{2,1,0:T(8,128)(2,1)}), bf16[768,24,256]{2,1,0:T(8,128)(2,1)}, u32[]{:S(2)}, u32[]{:S(2)}) %all-to-all-start.4) | async-done | bytes 9437216 | tf_op jit(solution)/shard_map/all_to_all | solution.py:29
  700.4 11.8 %convert_bitcast_fusion = f32[4,192,3,8,256]{4,3,2,1,0:T(8,128)} fusion(bf16[4,192,24,256]{3,2,1,0:T(8,128)(2,1)} %bitcast.22), kind=kLoop, calls=%fused_computation | loop fusion | flops 4718592 | bytes 28311552
  712.2 15.1 %copy.60 = f32[4,192,3,8,256]{4,3,0,2,1:T(8,128)} copy(f32[4,192,3,8,256]{4,3,2,1,0:T(8,128)} %convert_bitcast_fusion) | data formatting | bytes 37748736 | tf_op jit(solution)/shard_map/convert_element_type | solution.py:31
  727.3 0.0 copy-done
  727.3 22.1 %add_convert_fusion = bf16[192,24,1024]{2,1,0:T(8,128)(2,1)} fusion(f32[192,24,1024]{2,1,0:T(8,128)} %bitcast.44, f32[192,24,1024]{2,1,0:T(8,128)} %reshape.14, bf16[192,24,1024]{2,1,0:T(8,128)(2,1)} %param.7, bf16[1024,1024]{1,0:T(8,128)(2,1)S(1)} %copy-done), kind=kOutput, calls=%fused_computation.2 | convolution fusion | flops 9677832192 | bytes 58720256 | tf_op jit(solution)/shard_map/dot_general | solution.py:9
Async XLA Ops:
  0.0 727.3 %copy-start = (bf16[1024,1024]{1,0:T(8,128)(2,1)S(1)}, bf16[1024,1024]{1,0:T(8,128)(2,1)}, u32[]{:S(2)}) copy-start(bf16[1024,1024]{1,0:T(8,128)(2,1)} %param.8) | copy-start | bytes 6291460
  300.8 8.6 %copy-start.1 = (bf16[768,768]{1,0:T(8,128)(2,1)S(1)}, bf16[768,768]{1,0:T(8,128)(2,1)}, u32[]{:S(2)}) copy-start(bf16[768,768]{1,0:T(8,128)(2,1)} %param.13) | copy-start | bytes 3538948
  335.6 132.6 %all-to-all-start.3 = ((bf16[24,768,256]{2,0,1:T(8,128)(2,1)}), bf16[24,768,256]{2,0,1:T(8,128)(2,1)}, u32[]{:S(2)}, u32[]{:S(2)}) async-start(bf16[24,768,256]{2,0,1:T(8,128)(2,1)} %copy.50), calls=%async_computation.3 | async-start | bytes 18874368 | tf_op jit(solution)/shard_map/all_to_all | solution.py:24
  340.8 15.9 %copy-start.2 = (bf16[768,768]{1,0:T(8,128)(2,1)S(1)}, bf16[768,768]{1,0:T(8,128)(2,1)}, u32[]{:S(2)}) copy-start(bf16[768,768]{1,0:T(8,128)(2,1)} %param.10) | copy-start | bytes 3538948
  340.8 15.9 %copy-start.3 = (f32[768]{0:T(1024)S(1)}, f32[768]{0:T(1024)}, u32[]{:S(2)}) copy-start(f32[768]{0:T(1024)} %param.12) | copy-start | bytes 9220
  340.8 15.9 %copy-start.4 = (f32[768]{0:T(1024)S(1)}, f32[768]{0:T(1024)}, u32[]{:S(2)}) copy-start(f32[768]{0:T(1024)} %param.11) | copy-start | bytes 9220
  468.2 120.5 %all-to-all-start.1 = ((bf16[768,24,256]{2,1,0:T(8,128)(2,1)}), bf16[768,24,256]{2,1,0:T(8,128)(2,1)}, u32[]{:S(2)}, u32[]{:S(2)}) async-start(bf16[768,24,256]{2,1,0:T(8,128)(2,1)} %copy.45), calls=%async_computation.1 | async-start | bytes 18874368 | tf_op jit(solution)/shard_map/all_to_all | solution.py:28
  588.7 111.7 %all-to-all-start.4 = ((bf16[768,24,256]{2,1,0:T(8,128)(2,1)}), bf16[768,24,256]{2,1,0:T(8,128)(2,1)}, u32[]{:S(2)}, u32[]{:S(2)}) async-start(bf16[768,24,256]{2,1,0:T(8,128)(2,1)} %bitcast.41), calls=%async_computation.4 | async-start | bytes 18874368 | tf_op jit(solution)/shard_map/all_to_all | solution.py:29
where the time goes:
time: 757 us; the launch traced here: 749 us
  blocking collectives  266 us (35%)
  waiting for transfers between devices  241 us (32%)
  local copies, waits for them, and re-layouts  156 us (21%)
  matrix products  49.4 us (7%)
  starting transfers between devices  25.5 us (3%)
  other arithmetic  11.8 us (2%)
    all_to_all x1, blocking collectives, per_device(): lax.all_to_all(scalar_field, 'row', split_axis=2, concat_axis=0, tiled=True)  149 us
    all_to_all x1, blocking collectives, per_device(): lax.all_to_all(pencil_y, 'col', split_axis=0, concat_axis=1, tiled=True)  117 us
    all_to_all x1, waiting for transfers between devices, per_device(): lax.all_to_all(y_term, 'row', split_axis=0, concat_axis=2, tiled=True)  95.5 us
    all_to_all x1, waiting for transfers between devices, per_device(): lax.all_to_all(z_full.astype(jnp.bfloat16), 'col', split_axis=1, concat_a...  84.8 us
    all_to_all x1, waiting for transfers between devices, per_device(): lax.all_to_all(z_in_y, 'row', split_axis=0, concat_axis=2, tiled=True)  61.1 us
    convert_element_type x3, local copies, waits for them, and re-layouts, per_device(): total = x_term + y_back.astype(jnp.float32) + z_back.astype(jnp.float32)  60 us
    all_to_all x2, local copies, waits for them, and re-layouts, per_device(): lax.all_to_all(scalar_field, 'row', split_axis=2, concat_axis=0, tiled=True)  33.3 us
    dot_general x1, matrix products, x_apply(): product = jnp.dot(flat, x_operator, preferred_element_type=jnp.float32)  22.1 us
  transfers between devices with their start and end apart: 3, of which 3 were waited for; matrix products, arithmetic and copies ran while one was open for 13% of the time, Pallas kernels for 0%

commit v1 on v0

v1 whole, which is shorter than its diff:
```python
import functools

import jax
import jax.numpy as jnp
from jax import lax
from jax.experimental import pallas as pl
from jax.experimental.pallas import tpu as pltpu
from jax.sharding import PartitionSpec as P

MESH = pl.DeviceIdType.MESH
BF16 = jnp.bfloat16
F32 = jnp.float32
LANES = 128
CHUNKS = 4
PLANE = 16
ROWS = 192
ZS = 24
YS = ROWS // PLANE
HALF = ZS // 2
NY = 4 * ROWS
NZ = 2 * PLANE * ZS


def exchange_kernel(
    field, y_op, z_op,
    total, traded, z_in, y_in, z_out,
    turn, staged, block, z_pencil, z_result, y_pencil, y_send, y_own, y_got, z_got, summed,
    lo_s, lo_r, zi_s, zi_r, g_s, g_l, g_r, zo_s, zo_l, zo_r, ys_s, ys_r, back_s, back_r, keep_l, load,
):
    row, col = lax.axis_index("row"), lax.axis_index("col")
    hi, core = row // 2, row % 2
    plane, lo = col // 2, col % 2
    pz, py = plane // 4, plane % 4
    upper = 1 - lax.rem(hi + lo, 2)
    mine, theirs = upper * (CHUNKS * LANES), (1 - upper) * (CHUNKS * LANES)
    other_lo = 1 - lo

    lo_peer = (row, plane * 2 + other_lo)
    sibling = (hi * 2 + 1 - core, col)
    far_same = ((1 - hi) * 2 + core, plane * 2 + other_lo)
    far_cross = ((1 - hi) * 2 + 1 - core, plane * 2 + other_lo)

    def plane_peer(k):
        return lax.rem(pz + k // 4, 4) * 4 + lax.rem(py + k % 4, 4)

    def lanes(start, i):
        return pl.ds(pl.multiple_of(start + i * LANES, LANES), LANES)

    def remote(src, dst, send, recv, device):
        return pltpu.make_async_remote_copy(
            src_ref=src, dst_ref=dst, send_sem=send, recv_sem=recv, device_id=device, device_id_type=MESH
        )

    def drain(ref, sem):
        pltpu.make_async_copy(ref, ref, sem).wait()

    def fetch(src, dst):
        copy = pltpu.make_async_copy(src, dst, load)
        copy.start()
        copy.wait()

    barrier = pltpu.get_barrier_semaphore()
    for peer in (lo_peer, sibling, far_same, far_cross):
        pl.semaphore_signal(barrier, inc=1, device_id=peer, device_id_type=MESH)

    @pl.loop(1, PLANE)
    def _(k):
        pl.semaphore_signal(barrier, inc=1, device_id=(row, plane_peer(k) * 2 + lo), device_id_type=MESH)

    pl.semaphore_wait(barrier, 4 + PLANE - 1)

    def part_of(i, own):
        return field.at[:, :, lanes(mine, i)] if own else traded.at[i]

    def send_z(i, own):
        source = part_of(i, own)
        z_half = lo if own else other_lo
        part = 0 if own else 1

        @pl.loop(1, PLANE)
        def _(k):
            to = plane_peer(k)
            remote(
                source.at[pl.ds(to * YS, YS)], z_in.at[i, :, plane, z_half],
                zi_s.at[i, part], zi_r.at[i], (row, to * 2 + lo),
            ).start()

        pltpu.make_async_copy(
            source.at[pl.ds(plane * YS, YS)], z_in.at[i, :, plane, z_half], zi_r.at[i]
        ).start()

    def send_y(i, own):
        part, z_half = (0, lo) if own else (1, other_lo)
        if not own:
            drain(staged.at[i, pl.ds(0, HALF)], g_l.at[i, 0])
            for n in range(3):
                drain(staged.at[i, pl.ds(0, HALF)], g_s.at[i, 0, n])
        fetch(part_of(i, own), block)

        @pl.loop(0, ROWS // 16)
        def _(j):
            turn[pl.ds(j * 16 * ZS, 16 * ZS)] = block[pl.ds(j * 16, 16)].astype(F32).reshape(16 * ZS, LANES)

        @pl.loop(0, ZS)
        def _(z):
            staged[i, z] = turn[pl.ds(z, ROWS, stride=ZS)].astype(BF16)

        keep, give = pl.ds(core * HALF, HALF), pl.ds((1 - core) * HALF, HALF)
        for n, (piece, peer) in enumerate(((keep, far_same), (give, far_cross), (give, sibling))):
            remote(
                staged.at[i, piece], y_in.at[i, z_half, :, row], g_s.at[i, part, n], g_r.at[i, z_half], peer
            ).start()
        pltpu.make_async_copy(staged.at[i, keep], y_in.at[i, z_half, :, row], g_l.at[i, part]).start()

    def do_z(i):
        slot = i % 2
        if i >= 2:
            for half in range(2):
                drain(z_out.at[i, half, pl.ds(0, YS)], zo_l.at[i - 2, half])
                drain(z_out.at[i, half, pl.ds(0, (PLANE - 1) * YS)], zo_s.at[i - 2, half])
        drain(z_in.at[i], zi_r.at[i])
        fetch(z_in.at[i], z_pencil)

        @pl.loop(0, YS // 2)
        def _(j):
            def points(y):
                return z_pencil[y].astype(F32).reshape(NZ, LANES).astype(BF16)

            pair = jnp.concatenate([points(2 * j), points(2 * j + 1)], axis=1)
            product = jnp.dot(z_op[...], pair, preferred_element_type=F32)
            for n in range(2):
                result = product[:, n * LANES:(n + 1) * LANES].reshape(PLANE, 2, ZS, LANES)
                z_result[slot, 2 * j + n] = result.astype(BF16)

        for half in (other_lo, lo):
            @pl.loop(1, PLANE)
            def _(k):
                to = plane_peer(k)
                remote(
                    z_result.at[slot, :, to, half], z_out.at[i, half, pl.ds(plane * YS, YS)],
                    zo_s.at[i, half], zo_r.at[i, half], (row, to * 2 + lo),
                ).start()

            pltpu.make_async_copy(
                z_result.at[slot, :, plane, half], z_out.at[i, half, pl.ds(plane * YS, YS)], zo_l.at[i, half]
            ).start()

    def do_y(i, own):
        part, half = (0, lo) if own else (1, other_lo)
        drain(y_in.at[i, half, :, pl.ds(0, 3)], g_r.at[i, half])
        if not own:
            drain(staged.at[i, pl.ds(0, HALF)], g_l.at[i, 1])
        fetch(y_in.at[i, half], y_pencil)

        @pl.loop(0, HALF // 2)
        def _(j):
            pair = jnp.concatenate(
                [y_pencil[2 * j].reshape(NY, LANES), y_pencil[2 * j + 1].reshape(NY, LANES)], axis=1
            )
            product = jnp.dot(y_op[...], pair, preferred_element_type=F32).astype(BF16)
            for n in range(2):
                y_own[i, part, 2 * j + n] = product[:ROWS, n * LANES:(n + 1) * LANES]
                y_send[i, part, 2 * j + n] = product[ROWS:, n * LANES:(n + 1) * LANES]

        remote(y_send.at[i, part], y_got.at[i, part], ys_s.at[i, part], ys_r.at[i, part], sibling).start()

    def combine(i, own):
        part, half = (0, lo) if own else (1, other_lo)
        drain(y_got.at[i, part], ys_r.at[i, part])
        drain(z_out.at[i, half, pl.ds(0, (PLANE - 1) * YS)], zo_r.at[i, half])
        if i >= 2:
            drain(z_out.at[i, half, pl.ds(0, YS)], zo_l.at[i, half])
        fetch(z_out.at[i, half], z_got)

        @pl.loop(0, HALF)
        def _(z):
            turn[pl.ds(core * HALF + z, ROWS, stride=ZS)] = y_own[i, part, z].astype(F32)
            turn[pl.ds((1 - core) * HALF + z, ROWS, stride=ZS)] = y_got[i, part, z].astype(F32)

        if own:
            drain(summed.at[i], back_s.at[i])

        @pl.loop(0, ROWS // 16)
        def _(j):
            rows = pl.ds(j * 16, 16)
            y_term = turn[pl.ds(j * 16 * ZS, 16 * ZS)].reshape(16, ZS, LANES)
            summed[i, rows] = (y_term + z_got[rows].astype(F32)).astype(BF16)

        if own:
            pltpu.make_async_copy(summed.at[i], total.at[:, :, lanes(mine, i)], keep_l.at[i]).start()
        else:
            remote(summed.at[i], total.at[:, :, lanes(mine, i)], back_s.at[i], back_r.at[i], lo_peer).start()

    def take(i):
        drain(traded.at[i], lo_r.at[i])
        send_z(i, False)
        send_y(i, False)

    for i in range(CHUNKS):
        remote(field.at[:, :, lanes(theirs, i)], traded.at[i], lo_s.at[i], lo_r.at[i], lo_peer).start()
        send_z(i, True)
        send_y(i, True)
    take(0)
    take(1)
    do_z(0)
    take(2)
    do_z(1)
    take(3)
    for i in range(CHUNKS):
        do_y(i, False)
        if i < 2:
            do_z(i + 2)
        combine(i, False)
    for i in range(CHUNKS):
        do_y(i, True)
        combine(i, True)

    for i in range(CHUNKS):
        drain(traded.at[i], lo_s.at[i])
        for part in range(2):
            drain(z_in.at[i, :, pl.ds(0, PLANE - 1), 0], zi_s.at[i, part])
            drain(y_send.at[i, part], ys_s.at[i, part])
        for n in range(3):
            drain(staged.at[i, pl.ds(0, HALF)], g_s.at[i, 1, n])
        if i >= 2:
            for half in range(2):
                drain(z_out.at[i, half, pl.ds(0, (PLANE - 1) * YS)], zo_s.at[i, half])
        drain(summed.at[i], keep_l.at[i])
        drain(summed.at[i], back_r.at[i])


def exchange(field, y_op, z_op):
    any_space, vmem = pl.BlockSpec(memory_space=pl.ANY), pl.BlockSpec(memory_space=pltpu.VMEM)
    shape = lambda *dims: jax.ShapeDtypeStruct(dims, BF16)
    dma = pltpu.SemaphoreType.DMA
    return pl.pallas_call(
        exchange_kernel,
        name="exchange",
        out_shape=(
            shape(ROWS, ZS, 2 * CHUNKS * LANES),
            shape(CHUNKS, ROWS, ZS, LANES),
            shape(CHUNKS, YS, PLANE, 2, ZS, LANES),
            shape(CHUNKS, 2, HALF, 4, ROWS, LANES),
            shape(CHUNKS, 2, ROWS, ZS, LANES),
        ),
        in_specs=[any_space, vmem, vmem],
        out_specs=(any_space,) * 5,
        scratch_shapes=[
            pltpu.VMEM((ROWS * ZS, LANES), F32),
            pltpu.VMEM((CHUNKS, ZS, ROWS, LANES), BF16),
            pltpu.VMEM((ROWS, ZS, LANES), BF16),
            pltpu.VMEM((YS, PLANE, 2, ZS, LANES), BF16),
            pltpu.VMEM((2, YS, PLANE, 2, ZS, LANES), BF16),
            pltpu.VMEM((HALF, 4, ROWS, LANES), BF16),
            pltpu.VMEM((CHUNKS, 2, HALF, ROWS, LANES), BF16),
            pltpu.VMEM((CHUNKS, 2, HALF, ROWS, LANES), BF16),
            pltpu.VMEM((CHUNKS, 2, HALF, ROWS, LANES), BF16),
            pltpu.VMEM((ROWS, ZS, LANES), BF16),
            pltpu.VMEM((CHUNKS, ROWS, ZS, LANES), BF16),
            dma((CHUNKS,)), dma((CHUNKS,)),
            dma((CHUNKS, 2)), dma((CHUNKS,)),
            dma((CHUNKS, 2, 3)), dma((CHUNKS, 2)), dma((CHUNKS, 2)),
            dma((CHUNKS, 2)), dma((CHUNKS, 2)), dma((CHUNKS, 2)),
            dma((CHUNKS, 2)), dma((CHUNKS, 2)),
            dma((CHUNKS,)), dma((CHUNKS,)),
            dma((CHUNKS,)), dma,
        ],
        compiler_params=pltpu.CompilerParams(
            collective_id=0, has_side_effects=True, vmem_limit_bytes=58 * 2**20
        ),
        cost_estimate=pl.CostEstimate(flops=14_500_000_000, bytes_accessed=100_000_000, transcendentals=0),
    )(field, y_op, z_op)[0]


def x_kernel(field, x_op, rest, out):
    rows = field.shape[0] * field.shape[1]
    flat = field[...].reshape(rows, field.shape[2])
    product = jnp.dot(flat, x_op[...], preferred_element_type=F32)
    out[...] = (product.reshape(out.shape) + rest[...].astype(F32)).astype(BF16)


def add_x(field, x_op, rest):
    nx = field.shape[2]
    step = 16
    tile = pl.BlockSpec((step, ZS, nx), lambda i: (i, 0, 0))
    return pl.pallas_call(
        x_kernel,
        name="x_term",
        grid=(ROWS // step,),
        in_specs=[tile, pl.BlockSpec((nx, nx), lambda i: (0, 0)), tile],
        out_specs=tile,
        out_shape=jax.ShapeDtypeStruct(field.shape, BF16),
        compiler_params=pltpu.CompilerParams(vmem_limit_bytes=48 * 2**20),
    )(field, x_op, rest)


def per_device(scalar_field, x_operator, y_second, y_first, y_stretch, y_curve, z_operator):
    row = lax.axis_index("row")

    def operator_rows(r):
        cut = lambda a, axis: lax.dynamic_slice_in_dim(a, r * ROWS, ROWS, axis)
        return (
            cut(y_stretch, 0)[None, :] * cut(y_second, 1).astype(F32)
            + cut(y_curve, 0)[None, :] * cut(y_first, 1).astype(F32)
        ).astype(BF16).T

    sibling = row + 1 - 2 * lax.rem(row, 2)
    y_op = jnp.concatenate([operator_rows(row), operator_rows(sibling)], axis=0)
    rest = exchange(scalar_field, y_op, z_operator.T)
    return add_x(scalar_field, x_operator, rest)


def solution(mesh):
    in_specs = (P("row", "col", None), P(), P(), P(), P(), P(), P())
    out_specs = P("row", "col", None)
    return jax.shard_map(
        per_device, mesh=mesh, in_specs=in_specs, out_specs=out_specs, check_vma=False
    )
```

time: 757 us -> 284 us (0.38)
  Pallas kernels: 0 us -> 276 us
  blocking collectives: 266 us -> 0 us
  waiting for transfers between devices: 241 us -> 0 us
  local copies, waits for them, and re-layouts: 156 us -> 5.94 us
  matrix products: 49.4 us -> 0 us
  starting transfers between devices: 25.5 us -> 0 us
  other arithmetic: 11.8 us -> 1.22 us
    pallas_call x0 -> x2, Pallas kernels: none -> 276 us  [the longest x1 258 us: exchange(): pl.pallas_call(exchange_kernel, name='exchange', out_shape=(shape(ROWS, Z...]
    all_to_all x2 -> x0, blocking collectives: 266 us -> none  [the longest x1 149 us: per_device(): lax.all_to_all(scalar_field, 'row', split_axis=2, concat_axis=0, tiled=True)]
    all_to_all x3 -> x0, waiting for transfers between devices: 241 us -> none  [the longest x1 95.5 us: per_device(): lax.all_to_all(y_term, 'row', split_axis=0, concat_axis=2, tiled=True)]
    convert_element_type x5 -> x0, local copies, waits for them, and re-layouts: 85.4 us -> none  [the longest x3 60 us: per_device(): total = x_term + y_back.astype(jnp.float32) + z_back.astype(jnp.float32)]
    all_to_all x4 -> x0, local copies, waits for them, and re-layouts: 52.3 us -> none  [the longest x2 33.3 us: per_device(): lax.all_to_all(scalar_field, 'row', split_axis=2, concat_axis=0, tiled=True)]
    dot_general x3 -> x0, matrix products: 49.4 us -> none  [the longest x1 22.1 us: x_apply(): product = jnp.dot(flat, x_operator, preferred_element_type=jnp.float32)]
    all_to_all x3 -> x0, starting transfers between devices: 25.5 us -> none  [the longest x1 14.5 us: per_device(): lax.all_to_all(y_term, 'row', split_axis=0, concat_axis=2, tiled=True)]
    unnamed x11 -> x9, local copies, waits for them, and re-layouts: 17.8 us -> 3.09 us
  transfers between devices with their start and end apart: 3 -> 0, of which waited for: 3 -> 0; matrix products, arithmetic and copies ran while one was open for 13% -> 0% of each run, Pallas kernels for 0% -> 0%
where the time goes in v1:
time: 284 us; the launch traced here: 283 us
  Pallas kernels  276 us (97%)
  local copies, waits for them, and re-layouts  5.94 us (2%)
    pallas_call x1, Pallas kernels, exchange(): pl.pallas_call(exchange_kernel, name='exchange', out_shape=(shape(ROWS, Z...  258 us
    pallas_call x1, Pallas kernels, add_x(): pl.pallas_call(x_kernel, name='x_term', grid=(ROWS // step,), in_specs=[t...  18 us

profile of v1, /device:TPU:0, one launch (start us, length us, event | category | flops | bytes accessed | tf_op | source)
XLA Modules:
  0.0 282.8 jit_solution(3247498582247854189)
XLA Ops:
  0.0 0.8 fusion.2
  0.8 0.0 copy-start.1
  0.8 2.5 copy.12
  3.3 0.0 copy-done.1
  3.3 2.0 constant_dynamic-slice_fusion.2
  5.3 0.2 copy.14
  5.5 0.2 copy.16
  5.6 0.2 copy.15
  5.8 0.2 fusion.1
  6.0 0.2 copy.13
  6.1 0.2 fusion
  6.3 0.9 pad_maximum_fusion.y_op
  7.2 0.0 copy-start
  7.2 257.5 %exchange.1 = (bf16[192,24,1024]{2,1,0:T(8,128)(2,1)}, bf16[4,192,24,128]{3,2,1,0:T(8,128)(2,1)}, bf16[4,12,16,2,24,128]{5,4,3,2,1,0:T(8,128)(2,1)}, bf16[4,2,12...) custom-call(bf16[192,24,1024]{2,1,0:T(8,128)(2,1)} %field.3, bf16[384,768]{1,0:T(8,128)(2,1)} %pad_maximum_fusion.y_op, ...), custom_call_target="tpu_custom_call" | custom-call | flops 14499999744 | bytes 100000000 | tf_op jit(solution)/shard_map/exchange/pallas_call | solution.py:236
  264.7 0.0 copy-done
  264.7 18.0 %x_term.1 = bf16[192,24,1024]{2,1,0:T(8,128)(2,1)} custom-call(bf16[192,24,1024]{2,1,0:T(8,128)(2,1)} %field.3, bf16[1024,1024]{1,0:T(8,128)(2,1)S(1)} %copy-done, bf16[192,24,1024]{2,1,0:T(8,128)(2,1)} %get-tuple-element.6.rest), custom_call_target="tpu_custom_call" | custom-call | tf_op jit(solution)/shard_map/x_term/pallas_call | solution.py:286
Async XLA Ops:
  0.8 2.5 copy-start.1
  7.2 257.5 %copy-start = (bf16[1024,1024]{1,0:T(8,128)(2,1)S(1)}, bf16[1024,1024]{1,0:T(8,128)(2,1)}, u32[]{:S(2)}) copy-start(bf16[1024,1024]{1,0:T(8,128)(2,1)} %x_op.1) | copy-start | bytes 6291460

commit v2 on v1

v2 whole, which is shorter than its diff:
```python
import jax
import jax.numpy as jnp
from jax import lax
from jax.experimental import pallas as pl
from jax.experimental.pallas import tpu as pltpu
from jax.sharding import PartitionSpec as P

MESH = pl.DeviceIdType.MESH
BF16 = jnp.bfloat16
F32 = jnp.float32
LANES = 128
CHUNKS = 4
PLANE = 16
ROWS = 192
ZS = 24
YS = ROWS // PLANE
HALF = ZS // 2
XS = 16
NY = 4 * ROWS
NZ = 2 * PLANE * ZS


def laplacian_kernel(
    field, x_source, y_second, y_first, y_stretch, y_curve, z_source,
    total, traded, z_in, y_in, z_out, back, x_term,
    x_op, y_parts, y_op, z_raw, z_op, x_tile, x_result, x_got,
    turn, staged, block, z_pencil, z_result, y_pencil, y_result, y_got, z_got, summed, final,
    lo_s, lo_r, zi_s, zi_r, g_s, g_l, g_r, zo_s, zo_r, ys_s, ys_r, back_s, back_r, keep_l, load, ops_l, x_l, x_s,
    x_g,
):
    row, col = lax.axis_index("row"), lax.axis_index("col")
    hi, core = row // 2, row % 2
    plane, lo = col // 2, col % 2
    pz, py = plane // 4, plane % 4
    upper = 1 - lax.rem(hi + lo, 2)
    mine, theirs = upper * (CHUNKS * LANES), (1 - upper) * (CHUNKS * LANES)
    other_lo = 1 - lo

    lo_peer = (row, plane * 2 + other_lo)
    sibling = (hi * 2 + 1 - core, col)
    far_same = ((1 - hi) * 2 + core, plane * 2 + other_lo)
    far_cross = ((1 - hi) * 2 + 1 - core, plane * 2 + other_lo)

    def plane_peer(k):
        k = lax.rem(k * 7, PLANE)
        return lax.rem(pz + k // 4, 4) * 4 + lax.rem(py + k % 4, 4)

    def lanes(start, i):
        return pl.ds(pl.multiple_of(start + i * LANES, LANES), LANES)

    def remote(src, dst, send, recv, device):
        return pltpu.make_async_remote_copy(
            src_ref=src, dst_ref=dst, send_sem=send, recv_sem=recv, device_id=device, device_id_type=MESH
        )

    def drain(ref, sem):
        pltpu.make_async_copy(ref, ref, sem).wait()

    def fetch(src, dst):
        copy = pltpu.make_async_copy(src, dst, load)
        copy.start()
        copy.wait()

    y_columns = pl.ds(pl.multiple_of(hi * (2 * ROWS), LANES), 2 * ROWS)
    loads = [
        pltpu.make_async_copy(source, target, ops_l.at[n])
        for n, (source, target) in enumerate((
            (x_source, x_op), (y_second.at[:, y_columns], y_parts.at[0]),
            (y_first.at[:, y_columns], y_parts.at[1]), (z_source, z_raw),
        ))
    ]
    for copy in loads:
        copy.start()

    barrier = pltpu.get_barrier_semaphore()
    for peer in (lo_peer, sibling, far_same, far_cross):
        pl.semaphore_signal(barrier, inc=1, device_id=peer, device_id_type=MESH)

    @pl.loop(1, PLANE)
    def _(k):
        pl.semaphore_signal(barrier, inc=1, device_id=(row, plane_peer(k) * 2 + lo), device_id_type=MESH)

    pl.semaphore_wait(barrier, 4 + PLANE - 1)

    def part_of(i, own):
        return field.at[:, :, lanes(mine, i)] if own else traded.at[i]

    def send_z(i, own):
        source = part_of(i, own)
        z_half = lo if own else other_lo
        part = 0 if own else 1

        @pl.loop(1, PLANE)
        def _(k):
            to = plane_peer(k)
            remote(
                source.at[pl.ds(to * YS, YS)], z_in.at[i, :, plane, z_half],
                zi_s.at[i, part], zi_r.at[i], (row, to * 2 + lo),
            ).start()

        pltpu.make_async_copy(
            source.at[pl.ds(plane * YS, YS)], z_in.at[i, :, plane, z_half], zi_r.at[i]
        ).start()

    def send_y(i, own):
        part, z_half = (0, lo) if own else (1, other_lo)
        if not own:
            drain(staged.at[i, pl.ds(0, HALF)], g_l.at[i, 0])
            for n in range(3):
                drain(staged.at[i, pl.ds(0, HALF)], g_s.at[i, 0, n])
        fetch(part_of(i, own), block)

        @pl.loop(0, ROWS // 16)
        def _(j):
            turn[pl.ds(j * 16 * ZS, 16 * ZS)] = block[pl.ds(j * 16, 16)].astype(F32).reshape(16 * ZS, LANES)

        @pl.loop(0, ZS)
        def _(z):
            staged[i, z] = turn[pl.ds(z, ROWS, stride=ZS)].astype(BF16)

        keep, give = pl.ds(core * HALF, HALF), pl.ds((1 - core) * HALF, HALF)
        for n, (piece, peer) in enumerate(((keep, far_same), (give, far_cross), (give, sibling))):
            remote(
                staged.at[i, piece], y_in.at[i, z_half, :, row], g_s.at[i, part, n], g_r.at[i, z_half], peer
            ).start()
        pltpu.make_async_copy(staged.at[i, keep], y_in.at[i, z_half, :, row], g_l.at[i, part]).start()

    def do_z(i):
        drain(z_in.at[i], zi_r.at[i])
        fetch(z_in.at[i], z_pencil)

        @pl.loop(0, YS // 2)
        def _(j):
            def points(y):
                return z_pencil[y].astype(F32).reshape(NZ, LANES).astype(BF16)

            pair = jnp.concatenate([points(2 * j), points(2 * j + 1)], axis=1)
            product = jnp.dot(z_op[...], pair, preferred_element_type=F32)
            for n in range(2):
                result = product[:, n * LANES:(n + 1) * LANES].reshape(PLANE, 2, ZS, LANES)
                z_result[i, 2 * j + n] = result.astype(BF16)

    def return_z(i, own):
        half = lo if own else other_lo

        @pl.loop(1, PLANE)
        def _(k):
            to = plane_peer(k)
            remote(
                z_result.at[i, :, to, half], z_out.at[i, half, pl.ds(plane * YS, YS)],
                zo_s.at[i, half], zo_r.at[i, half], (row, to * 2 + lo),
            ).start()

        pltpu.make_async_copy(
            z_result.at[i, :, plane, half], z_out.at[i, half, pl.ds(plane * YS, YS)], zo_r.at[i, half]
        ).start()

    def make_y_op():
        loads[1].wait()
        loads[2].wait()
        for n in range(3):
            here = slice(n * LANES, (n + 1) * LANES)
            there = pl.ds(pl.multiple_of(hi * (2 * ROWS) + n * LANES, LANES), LANES)
            combined = (
                y_stretch[:, there] * y_parts[0, :, here].astype(F32)
                + y_curve[:, there] * y_parts[1, :, here].astype(F32)
            )
            y_op[here] = combined.T.astype(BF16)

    def make_z_op():
        loads[3].wait()
        for n in range(NZ // LANES):
            here = slice(n * LANES, (n + 1) * LANES)
            z_op[here] = z_raw[:, here].astype(F32).T.astype(BF16)

    def x_load(j, slot):
        return pltpu.make_async_copy(field.at[pl.ds(j * XS, XS)], x_tile.at[slot], x_l.at[slot])

    def x_store(j, slot):
        return pltpu.make_async_copy(x_result.at[slot], x_term.at[:, pl.ds(j * XS, XS)], x_s.at[slot])

    def do_x(first, last):
        @pl.loop(first, last)
        def _(j):
            slot = lax.rem(j, 2)
            x_load(j, slot).wait()

            @pl.when(j + 1 < ROWS // XS)
            def _():
                x_load(j + 1, 1 - slot).start()

            @pl.when(j >= 2)
            def _():
                x_store(j - 2, slot).wait()

            flat = x_tile[slot].reshape(XS * ZS, 2 * CHUNKS * LANES)
            product = jnp.dot(flat, x_op[...], preferred_element_type=F32)
            for n in range(2 * CHUNKS):
                x_result[slot, n] = product[:, n * LANES:(n + 1) * LANES].reshape(XS, ZS, LANES)
            x_store(j, slot).start()

    def do_y(i, own):
        part, half = (0, lo) if own else (1, other_lo)
        drain(y_in.at[i, half, :, pl.ds(0, 3)], g_r.at[i, half])
        if not own:
            drain(staged.at[i, pl.ds(0, HALF)], g_l.at[i, 1])
        fetch(y_in.at[i, half], y_pencil)

        @pl.loop(0, HALF // 2)
        def _(j):
            pair = jnp.concatenate(
                [y_pencil[2 * j].reshape(NY, LANES), y_pencil[2 * j + 1].reshape(NY, LANES)], axis=1
            )
            product = jnp.dot(y_op[...], pair, preferred_element_type=F32).astype(BF16)
            for n in range(2):
                for c in range(2):
                    y_result[i, part, c, 2 * j + n] = product[c * ROWS:(c + 1) * ROWS, n * LANES:(n + 1) * LANES]

        remote(
            y_result.at[i, part, 1 - core], y_got.at[i, part], ys_s.at[i, part], ys_r.at[i, part], sibling
        ).start()

    def x_fetch(i, own):
        return pltpu.make_async_copy(x_term.at[(upper if own else 1 - upper) * CHUNKS + i], x_got, x_g)

    order = [(0, False), (1, False), (0, True), (2, False), (1, True), (2, True), (3, False), (3, True)]

    def keep(i, own):
        n = order.index((i, own)) % 2
        return pltpu.make_async_copy(
            final.at[n], total.at[:, :, lanes(mine if own else theirs, i)], keep_l.at[n]
        )

    def slot_for(i, own):
        n = order.index((i, own))
        if n >= 2:
            keep(*order[n - 2]).wait()
        return n % 2

    def combine(i, own):
        part, half = (0, lo) if own else (1, other_lo)
        if own:
            x_fetch(i, True).start()
        drain(y_got.at[i, part], ys_r.at[i, part])

        @pl.loop(0, HALF)
        def _(z):
            turn[pl.ds(core * HALF + z, ROWS, stride=ZS)] = y_result[i, part, core, z].astype(F32)
            turn[pl.ds((1 - core) * HALF + z, ROWS, stride=ZS)] = y_got[i, part, z].astype(F32)

        drain(z_out.at[i, half], zo_r.at[i, half])
        fetch(z_out.at[i, half], z_got)
        if own:
            x_fetch(i, True).wait()
            slot = slot_for(i, True)

        @pl.loop(0, ROWS // 16)
        def _(j):
            rows = pl.ds(j * 16, 16)
            both = turn[pl.ds(j * 16 * ZS, 16 * ZS)].reshape(16, ZS, LANES) + z_got[rows].astype(F32)
            if own:
                final[slot, rows] = (both + x_got[rows]).astype(BF16)
            else:
                summed[i, rows] = both.astype(BF16)

        if own:
            keep(i, True).start()
        else:
            remote(summed.at[i], back.at[i], back_s.at[i], back_r.at[i], lo_peer).start()

    def finish(i):
        x_fetch(i, False).start()
        drain(back.at[i], back_r.at[i])
        fetch(back.at[i], z_got)
        x_fetch(i, False).wait()
        slot = slot_for(i, False)

        @pl.loop(0, ROWS // 16)
        def _(j):
            rows = pl.ds(j * 16, 16)
            final[slot, rows] = (z_got[rows].astype(F32) + x_got[rows]).astype(BF16)

        keep(i, False).start()

    def take(i):
        drain(traded.at[i], lo_r.at[i])
        send_z(i, False)
        send_y(i, False)

    for i in range(CHUNKS):
        remote(field.at[:, :, lanes(theirs, i)], traded.at[i], lo_s.at[i], lo_r.at[i], lo_peer).start()
    x_load(0, 0).start()
    send_z(0, True)
    send_y(0, True)
    send_z(1, True)
    send_z(2, True)
    for i in range(1, CHUNKS):
        send_y(i, True)
    loads[0].wait()
    do_x(0, 6)
    take(0)
    make_y_op()
    make_z_op()
    do_y(0, False)
    do_x(6, 12)
    for slot in range(2):
        x_store(slot, slot).wait()
    take(1)
    do_z(0)
    return_z(0, False)
    send_z(3, True)
    do_y(1, False)
    take(2)
    do_z(1)
    return_z(1, False)
    combine(0, False)
    do_y(2, False)
    take(3)
    do_z(2)
    return_z(2, False)
    combine(1, False)
    do_z(3)
    return_z(3, False)
    for i in range(CHUNKS):
        return_z(i, True)
    do_y(3, False)
    finish(0)
    do_y(0, True)
    combine(2, False)
    combine(3, False)
    finish(1)
    do_y(1, True)
    combine(0, True)
    finish(2)
    do_y(2, True)
    combine(1, True)
    combine(2, True)
    do_y(3, True)
    finish(3)
    combine(3, True)

    for i in range(CHUNKS):
        drain(traded.at[i], lo_s.at[i])
        for part in range(2):
            drain(z_in.at[i, :, pl.ds(0, PLANE - 1), 0], zi_s.at[i, part])
            drain(y_got.at[i, part], ys_s.at[i, part])
        for n in range(3):
            drain(staged.at[i, pl.ds(0, HALF)], g_s.at[i, 1, n])
        for half in range(2):
            drain(z_out.at[i, half, pl.ds(0, (PLANE - 1) * YS)], zo_s.at[i, half])
        drain(summed.at[i], back_s.at[i])
    for block_id in order[-2:]:
        keep(*block_id).wait()


def laplacian(*operands):
    any_space, vmem = pl.BlockSpec(memory_space=pl.ANY), pl.BlockSpec(memory_space=pltpu.VMEM)
    shape = lambda *dims: jax.ShapeDtypeStruct(dims, BF16)
    held = lambda *dims: pltpu.VMEM(dims, BF16)
    dma = pltpu.SemaphoreType.DMA
    nx = 2 * CHUNKS * LANES
    return pl.pallas_call(
        laplacian_kernel,
        name="laplacian",
        out_shape=(
            shape(ROWS, ZS, nx),
            shape(CHUNKS, ROWS, ZS, LANES),
            shape(CHUNKS, YS, PLANE, 2, ZS, LANES),
            shape(CHUNKS, 2, HALF, 4, ROWS, LANES),
            shape(CHUNKS, 2, ROWS, ZS, LANES),
            shape(CHUNKS, ROWS, ZS, LANES),
            jax.ShapeDtypeStruct((2 * CHUNKS, ROWS, ZS, LANES), F32),
        ),
        in_specs=[any_space] * 4 + [vmem] * 2 + [any_space],
        out_specs=(any_space,) * 7,
        scratch_shapes=[
            held(nx, nx), held(2, NY, 2 * ROWS), held(2 * ROWS, NY), held(NZ, NZ), held(NZ, NZ),
            held(2, XS, ZS, nx),
            pltpu.VMEM((2, 2 * CHUNKS, XS, ZS, LANES), F32),
            pltpu.VMEM((ROWS, ZS, LANES), F32),
            pltpu.VMEM((ROWS * ZS, LANES), F32),
            held(CHUNKS, ZS, ROWS, LANES),
            held(ROWS, ZS, LANES),
            held(YS, PLANE, 2, ZS, LANES),
            held(CHUNKS, YS, PLANE, 2, ZS, LANES),
            held(HALF, 4, ROWS, LANES),
            held(CHUNKS, 2, 2, HALF, ROWS, LANES),
            held(CHUNKS, 2, HALF, ROWS, LANES),
            held(ROWS, ZS, LANES),
            held(CHUNKS, ROWS, ZS, LANES),
            held(2, ROWS, ZS, LANES),
            dma((CHUNKS,)), dma((CHUNKS,)),
            dma((CHUNKS, 2)), dma((CHUNKS,)),
            dma((CHUNKS, 2, 3)), dma((CHUNKS, 2)), dma((CHUNKS, 2)),
            dma((CHUNKS, 2)), dma((CHUNKS, 2)),
            dma((CHUNKS, 2)), dma((CHUNKS, 2)),
            dma((CHUNKS,)), dma((CHUNKS,)),
            dma((2,)), dma, dma((4,)), dma((2,)), dma((2,)), dma,
        ],
        compiler_params=pltpu.CompilerParams(
            collective_id=0, has_side_effects=True, vmem_limit_bytes=62 * 2**20
        ),
        cost_estimate=pl.CostEstimate(flops=24_200_000_000, bytes_accessed=180_000_000, transcendentals=0),
    )(*operands)[0]


def copy_kernel(source, target, held, read, written):
    parts = read.shape[0]
    rows = source.shape[0] // parts
    piece = lambda n: pl.ds(n * rows, rows)
    reads = [pltpu.make_async_copy(source.at[piece(n)], held.at[piece(n)], read.at[n]) for n in range(parts)]
    writes = [pltpu.make_async_copy(held.at[piece(n)], target.at[piece(n)], written.at[n]) for n in range(parts)]
    for copy in reads:
        copy.start()
    for n in range(parts):
        reads[n].wait()
        writes[n].start()
    for copy in writes:
        copy.wait()


def copied(array):
    any_space = pl.BlockSpec(memory_space=pl.ANY)
    parts = 12
    return pl.pallas_call(
        copy_kernel,
        name="result",
        in_specs=[any_space],
        out_specs=any_space,
        out_shape=jax.ShapeDtypeStruct(array.shape, array.dtype),
        scratch_shapes=[
            pltpu.VMEM(array.shape, array.dtype),
            pltpu.SemaphoreType.DMA((parts,)), pltpu.SemaphoreType.DMA((parts,)),
        ],
        compiler_params=pltpu.CompilerParams(vmem_limit_bytes=60 * 2**20),
    )(array)


def per_device(scalar_field, x_operator, y_second, y_first, y_stretch, y_curve, z_operator):
    return copied(laplacian(
        scalar_field, x_operator, y_second, y_first, y_stretch[None, :], y_curve[None, :], z_operator
    ))


def solution(mesh):
    in_specs = (P("row", "col", None), P(), P(), P(), P(), P(), P())
    out_specs = P("row", "col", None)
    return jax.shard_map(
        per_device, mesh=mesh, in_specs=in_specs, out_specs=out_specs, check_vma=False
    )
```

time: 284 us -> 242 us (0.85)
  Pallas kernels: 276 us -> 238 us
  local copies, waits for them, and re-layouts: 5.94 us -> 2.53 us
    pallas_call x2, Pallas kernels: 276 us -> 238 us  [the longest x1 231 us: laplacian(): pl.pallas_call(laplacian_kernel, name='laplacian', out_shape=(shape(ROWS,...]
    unnamed x9 -> x0, local copies, waits for them, and re-layouts: 3.09 us -> none
    dynamic_slice x2 -> x0, local copies, waits for them, and re-layouts: 2.85 us -> none  [operator_rows(): cut = lambda a, axis: lax.dynamic_slice_in_dim(a, r * ROWS, ROWS, axis)]
where the time goes in v2:
time: 242 us; the launch traced here: 240 us
  Pallas kernels  238 us (98%)
  local copies, waits for them, and re-layouts  2.53 us (1%)
    pallas_call x1, Pallas kernels, laplacian(): pl.pallas_call(laplacian_kernel, name='laplacian', out_shape=(shape(ROWS,...  231 us
    pallas_call x1, Pallas kernels, copied(): pl.pallas_call(copy_kernel, name='result', in_specs=[any_space], out_spec...  7.27 us

profile of v2, /device:TPU:0, one launch (start us, length us, event | category | flops | bytes accessed | tf_op | source)
XLA Modules:
  0.0 240.3 jit_solution(15724552523467611948)
XLA Ops:
  0.0 1.3 broadcast_in_dim.6.y_stretch
  1.3 1.3 broadcast_in_dim.7.y_curve
  2.5 230.5 %laplacian.1 = (bf16[192,24,1024]{2,1,0:T(8,128)(2,1)}, bf16[4,192,24,128]{3,2,1,0:T(8,128)(2,1)}, bf16[4,12,16,2,24,128]{5,4,3,2,1,0:T(8,128)(2,1)}, bf16[4,2,1...) custom-call(bf16[192,24,1024]{2,1,0:T(8,128)(2,1)} %field.1, ...), custom_call_target="tpu_custom_call" | custom-call | flops 24199999488 | bytes 180000000 | tf_op jit(solution)/shard_map/laplacian/pallas_call | solution.py:362
  233.1 7.3 %result.1 = bf16[192,24,1024]{2,1,0:T(8,128)(2,1)} custom-call(bf16[192,24,1024]{2,1,0:T(8,128)(2,1)} %get-tuple-element.6.source), custom_call_target="tpu_custom_call" | custom-call | tf_op jit(solution)/shard_map/result/pallas_call | solution.py:425

commit v3 on v2

--- a/solution.py
+++ b/solution.py
@@ -15,18 +15,21 @@
 ZS = 24
 YS = ROWS // PLANE
 HALF = ZS // 2
-XS = 16
+QUARTER = HALF // 2
+LAST = CHUNKS - 1
+XS = 8
 NY = 4 * ROWS
 NZ = 2 * PLANE * ZS
 
 
 def laplacian_kernel(
     field, x_source, y_second, y_first, y_stretch, y_curve, z_source,
-    total, traded, z_in, y_in, z_out, back, x_term,
+    total, traded, z_in, y_in, z_out, x_term,
     x_op, y_parts, y_op, z_raw, z_op, x_tile, x_result, x_got,
     turn, staged, block, z_pencil, z_result, y_pencil, y_result, y_got, z_got, summed, final,
+    back, y_last, z_last,
     lo_s, lo_r, zi_s, zi_r, g_s, g_l, g_r, zo_s, zo_r, ys_s, ys_r, back_s, back_r, keep_l, load, ops_l, x_l, x_s,
-    x_g,
+    x_g, z_l, last_r, last_ys_s, last_ys_r,
 ):
     row, col = lax.axis_index("row"), lax.axis_index("col")
     hi, core = row // 2, row % 2
@@ -72,6 +75,9 @@
     for copy in loads:
         copy.start()
 
+    def x_load(j, slot):
+        return pltpu.make_async_copy(field.at[pl.ds(j * XS, XS)], x_tile.at[slot], x_l.at[slot])
+
     barrier = pltpu.get_barrier_semaphore()
     for peer in (lo_peer, sibling, far_same, far_cross):
         pl.semaphore_signal(barrier, inc=1, device_id=peer, device_id_type=MESH)
@@ -80,6 +86,9 @@
     def _(k):
         pl.semaphore_signal(barrier, inc=1, device_id=(row, plane_peer(k) * 2 + lo), device_id_type=MESH)
 
+    first_block = pltpu.make_async_copy(field.at[:, :, lanes(mine, 0)], block, load)
+    first_block.start()
+    x_load(0, 0).start()
     pl.semaphore_wait(barrier, 4 + PLANE - 1)
 
     def part_of(i, own):
@@ -102,13 +111,23 @@
             source.at[pl.ds(plane * YS, YS)], z_in.at[i, :, plane, z_half], zi_r.at[i]
         ).start()
 
+    def y_target(i, z_half, own, source_row):
+        held = y_last if i == LAST and own else y_in.at[i, z_half]
+        return held.at[:, source_row]
+
+    def z_target(i, half, own):
+        return z_last if i == LAST and own else z_out.at[i, half]
+
     def send_y(i, own):
         part, z_half = (0, lo) if own else (1, other_lo)
         if not own:
             drain(staged.at[i, pl.ds(0, HALF)], g_l.at[i, 0])
             for n in range(3):
                 drain(staged.at[i, pl.ds(0, HALF)], g_s.at[i, 0, n])
-        fetch(part_of(i, own), block)
+        if own and i == 0:
+            first_block.wait()
+        else:
+            fetch(part_of(i, own), block)
 
         @pl.loop(0, ROWS // 16)
         def _(j):
@@ -118,12 +137,24 @@
         def _(z):
             staged[i, z] = turn[pl.ds(z, ROWS, stride=ZS)].astype(BF16)
 
-        keep, give = pl.ds(core * HALF, HALF), pl.ds((1 - core) * HALF, HALF)
-        for n, (piece, peer) in enumerate(((keep, far_same), (give, far_cross), (give, sibling))):
+        keep, give = core * HALF, (1 - core) * HALF
+        whole = pl.ds(0, HALF)
+        near = y_target(i, z_half, own, row)
+        far = y_target(i, z_half, not own, row)
+        pieces = [(keep, far_same, 0, far), (give, far_cross, 1, far), (give, sibling, 2, near)]
+        if i == LAST and not own:
+            for h in range(2):
+                for z, peer, n, target in pieces[:2]:
+                    remote(
+                        staged.at[i, pl.ds(z + h * QUARTER, QUARTER)], target.at[pl.ds(h * QUARTER, QUARTER)],
+                        g_s.at[i, part, n], last_r.at[h], peer,
+                    ).start()
+            pieces = pieces[2:]
+        for z, peer, n, target in pieces:
             remote(
-                staged.at[i, piece], y_in.at[i, z_half, :, row], g_s.at[i, part, n], g_r.at[i, z_half], peer
+                staged.at[i, pl.ds(z, HALF)], target.at[whole], g_s.at[i, part, n], g_r.at[i, z_half], peer
             ).start()
-        pltpu.make_async_copy(staged.at[i, keep], y_in.at[i, z_half, :, row], g_l.at[i, part]).start()
+        pltpu.make_async_copy(staged.at[i, pl.ds(keep, HALF)], near.at[whole], g_l.at[i, part]).start()
 
     def do_z(i):
         drain(z_in.at[i], zi_r.at[i])
@@ -142,17 +173,18 @@
 
     def return_z(i, own):
         half = lo if own else other_lo
+        target = z_target(i, half, own).at[pl.ds(plane * YS, YS)]
 
         @pl.loop(1, PLANE)
         def _(k):
             to = plane_peer(k)
             remote(
-                z_result.at[i, :, to, half], z_out.at[i, half, pl.ds(plane * YS, YS)],
+                z_result.at[i, :, to, half], target,
                 zo_s.at[i, half], zo_r.at[i, half], (row, to * 2 + lo),
             ).start()
 
         pltpu.make_async_copy(
-            z_result.at[i, :, plane, half], z_out.at[i, half, pl.ds(plane * YS, YS)], zo_r.at[i, half]
+            z_result.at[i, :, plane, half], target, zo_r.at[i, half]
         ).start()
 
     def make_y_op():
@@ -162,8 +194,8 @@
             here = slice(n * LANES, (n + 1) * LANES)
             there = pl.ds(pl.multiple_of(hi * (2 * ROWS) + n * LANES, LANES), LANES)
             combined = (
-                y_stretch[:, there] * y_parts[0, :, here].astype(F32)
-                + y_curve[:, there] * y_parts[1, :, here].astype(F32)
+                y_stretch[there].reshape(1, LANES) * y_parts[0, :, here].astype(F32)
+                + y_curve[there].reshape(1, LANES) * y_parts[1, :, here].astype(F32)
             )
             y_op[here] = combined.T.astype(BF16)
 
@@ -173,9 +205,6 @@
             here = slice(n * LANES, (n + 1) * LANES)
             z_op[here] = z_raw[:, here].astype(F32).T.astype(BF16)
 
-    def x_load(j, slot):
-        return pltpu.make_async_copy(field.at[pl.ds(j * XS, XS)], x_tile.at[slot], x_l.at[slot])
-
     def x_store(j, slot):
         return pltpu.make_async_copy(x_result.at[slot], x_term.at[:, pl.ds(j * XS, XS)], x_s.at[slot])
 
@@ -199,25 +228,37 @@
                 x_result[slot, n] = product[:, n * LANES:(n + 1) * LANES].reshape(XS, ZS, LANES)
             x_store(j, slot).start()
 
+    def y_products(i, held, first, last):
+        @pl.loop(first, last)
+        def _(j):
+            pair = jnp.concatenate([held[2 * j].reshape(NY, LANES), held[2 * j + 1].reshape(NY, LANES)], axis=1)
+            product = jnp.dot(y_op[...], pair, preferred_element_type=F32).astype(BF16)
+            for n in range(2):
+                for c in range(2):
+                    y_result[i, c, 2 * j + n] = product[c * ROWS:(c + 1) * ROWS, n * LANES:(n + 1) * LANES]
+
     def do_y(i, own):
         part, half = (0, lo) if own else (1, other_lo)
         drain(y_in.at[i, half, :, pl.ds(0, 3)], g_r.at[i, half])
-        if not own:
+        if own:
+            drain(y_got.at[i, 1], ys_s.at[i, 1])
+        else:
             drain(staged.at[i, pl.ds(0, HALF)], g_l.at[i, 1])
         fetch(y_in.at[i, half], y_pencil)
-
-        @pl.loop(0, HALF // 2)
-        def _(j):
-            pair = jnp.concatenate(
-                [y_pencil[2 * j].reshape(NY, LANES), y_pencil[2 * j + 1].reshape(NY, LANES)], axis=1
-            )
-            product = jnp.dot(y_op[...], pair, preferred_element_type=F32).astype(BF16)
-            for n in range(2):
-                for c in range(2):
-                    y_result[i, part, c, 2 * j + n] = product[c * ROWS:(c + 1) * ROWS, n * LANES:(n + 1) * LANES]
-
+        y_products(i, y_pencil, 0, HALF // 2)
         remote(
-            y_result.at[i, part, 1 - core], y_got.at[i, part], ys_s.at[i, part], ys_r.at[i, part], sibling
+            y_result.at[i, 1 - core], y_got.at[i, part], ys_s.at[i, part], ys_r.at[i, part], sibling
+        ).start()
+
+    def do_y_last(h):
+        if h == 0:
+            drain(y_got.at[LAST, 1], ys_s.at[LAST, 1])
+            drain(y_last.at[:, 0], g_r.at[LAST, lo])
+        drain(y_last.at[pl.ds(0, QUARTER), pl.ds(0, 2)], last_r.at[h])
+        y_products(LAST, y_last, h * (QUARTER // 2), (h + 1) * (QUARTER // 2))
+        piece = pl.ds(h * QUARTER, QUARTER)
+        remote(
+            y_result.at[LAST, 1 - core, piece], y_got.at[LAST, 0, piece], last_ys_s.at[h], last_ys_r.at[h], sibling
         ).start()
 
     def x_fetch(i, own):
@@ -225,62 +266,78 @@
 
     order = [(0, False), (1, False), (0, True), (2, False), (1, True), (2, True), (3, False), (3, True)]
 
-    def keep(i, own):
-        n = order.index((i, own)) % 2
+    def keep_rows(i, own, first):
+        n, rows = order.index((i, own)) % 2, pl.ds(first, ROWS // 2)
         return pltpu.make_async_copy(
-            final.at[n], total.at[:, :, lanes(mine if own else theirs, i)], keep_l.at[n]
+            final.at[n, rows], total.at[rows, :, lanes(mine if own else theirs, i)], keep_l.at[n]
         )
 
     def slot_for(i, own):
         n = order.index((i, own))
         if n >= 2:
-            keep(*order[n - 2]).wait()
+            drain(final.at[n % 2], keep_l.at[n % 2])
         return n % 2
 
     def combine(i, own):
         part, half = (0, lo) if own else (1, other_lo)
+        last = own and i == LAST
         if own:
             x_fetch(i, True).start()
-        drain(y_got.at[i, part], ys_r.at[i, part])
 
         @pl.loop(0, HALF)
         def _(z):
-            turn[pl.ds(core * HALF + z, ROWS, stride=ZS)] = y_result[i, part, core, z].astype(F32)
+            turn[pl.ds(core * HALF + z, ROWS, stride=ZS)] = y_result[i, core, z].astype(F32)
+
+        if last:
+            z_term = z_last
+            for h in range(2):
+                drain(y_got.at[i, 0, pl.ds(0, QUARTER)], last_ys_r.at[h])
+        else:
+            z_term = z_got
+            drain(z_out.at[i, half], zo_r.at[i, half])
+            z_fetch = pltpu.make_async_copy(z_out.at[i, half], z_got, z_l)
+            z_fetch.start()
+            drain(y_got.at[i, part], ys_r.at[i, part])
+
+        @pl.loop(0, HALF)
+        def _(z):
             turn[pl.ds((1 - core) * HALF + z, ROWS, stride=ZS)] = y_got[i, part, z].astype(F32)
 
-        drain(z_out.at[i, half], zo_r.at[i, half])
-        fetch(z_out.at[i, half], z_got)
         if own:
             x_fetch(i, True).wait()
             slot = slot_for(i, True)
-
-        @pl.loop(0, ROWS // 16)
-        def _(j):
-            rows = pl.ds(j * 16, 16)
-            both = turn[pl.ds(j * 16 * ZS, 16 * ZS)].reshape(16, ZS, LANES) + z_got[rows].astype(F32)
+        if last:
+            drain(z_last, zo_r.at[i, half])
+        else:
+            z_fetch.wait()
+        for first in (0, ROWS // 2):
+            @pl.loop(0, ROWS // 32)
+            def _(j):
+                rows = pl.ds(first + j * 16, 16)
+                both = turn[pl.ds((first + j * 16) * ZS, 16 * ZS)].reshape(16, ZS, LANES) + z_term[rows].astype(F32)
+                if own:
+                    final[slot, rows] = (both + x_got[rows]).astype(BF16)
+                else:
+                    summed[i, rows] = both.astype(BF16)
+
             if own:
-                final[slot, rows] = (both + x_got[rows]).astype(BF16)
-            else:
-                summed[i, rows] = both.astype(BF16)
-
-        if own:
-            keep(i, True).start()
-        else:
+                keep_rows(i, True, first).start()
+
+        if not own:
             remote(summed.at[i], back.at[i], back_s.at[i], back_r.at[i], lo_peer).start()
 
     def finish(i):
         x_fetch(i, False).start()
         drain(back.at[i], back_r.at[i])
-        fetch(back.at[i], z_got)
         x_fetch(i, False).wait()
         slot = slot_for(i, False)
-
-        @pl.loop(0, ROWS // 16)
-        def _(j):
-            rows = pl.ds(j * 16, 16)
-            final[slot, rows] = (z_got[rows].astype(F32) + x_got[rows]).astype(BF16)
-
-        keep(i, False).start()
+        for first in (0, ROWS // 2):
+            @pl.loop(0, ROWS // 32)
+            def _(j):
+                rows = pl.ds(first + j * 16, 16)
+                final[slot, rows] = (back[i, rows].astype(F32) + x_got[rows]).astype(BF16)
+
+            keep_rows(i, False, first).start()
 
     def take(i):
         drain(traded.at[i], lo_r.at[i])
@@ -289,7 +346,6 @@
 
     for i in range(CHUNKS):
         remote(field.at[:, :, lanes(theirs, i)], traded.at[i], lo_s.at[i], lo_r.at[i], lo_peer).start()
-    x_load(0, 0).start()
     send_z(0, True)
     send_y(0, True)
     send_z(1, True)
@@ -297,12 +353,13 @@
     for i in range(1, CHUNKS):
         send_y(i, True)
     loads[0].wait()
-    do_x(0, 6)
+    steps = ROWS // XS
+    do_x(0, steps // 2)
     take(0)
     make_y_op()
     make_z_op()
     do_y(0, False)
-    do_x(6, 12)
+    do_x(steps // 2, steps)
     for slot in range(2):
         x_store(slot, slot).wait()
     take(1)
@@ -334,8 +391,9 @@
     finish(2)
     do_y(2, True)
     combine(1, True)
+    do_y_last(0)
     combine(2, True)
-    do_y(3, True)
+    do_y_last(1)
     finish(3)
     combine(3, True)
 
@@ -343,14 +401,16 @@
         drain(traded.at[i], lo_s.at[i])
         for part in range(2):
             drain(z_in.at[i, :, pl.ds(0, PLANE - 1), 0], zi_s.at[i, part])
-            drain(y_got.at[i, part], ys_s.at[i, part])
         for n in range(3):
             drain(staged.at[i, pl.ds(0, HALF)], g_s.at[i, 1, n])
         for half in range(2):
             drain(z_out.at[i, half, pl.ds(0, (PLANE - 1) * YS)], zo_s.at[i, half])
+        if i != LAST:
+            drain(y_got.at[i, 0], ys_s.at[i, 0])
         drain(summed.at[i], back_s.at[i])
-    for block_id in order[-2:]:
-        keep(*block_id).wait()
+    for n in range(2):
+        drain(final.at[n], keep_l.at[n])
+        drain(y_got.at[LAST, 0, pl.ds(0, QUARTER)], last_ys_s.at[n])
 
 
 def laplacian(*operands):
@@ -368,11 +428,10 @@
             shape(CHUNKS, YS, PLANE, 2, ZS, LANES),
             shape(CHUNKS, 2, HALF, 4, ROWS, LANES),
             shape(CHUNKS, 2, ROWS, ZS, LANES),
-            shape(CHUNKS, ROWS, ZS, LANES),
             jax.ShapeDtypeStruct((2 * CHUNKS, ROWS, ZS, LANES), F32),
         ),
         in_specs=[any_space] * 4 + [vmem] * 2 + [any_space],
-        out_specs=(any_space,) * 7,
+        out_specs=(any_space,) * 6,
         scratch_shapes=[
             held(nx, nx), held(2, NY, 2 * ROWS), held(2 * ROWS, NY), held(NZ, NZ), held(NZ, NZ),
             held(2, XS, ZS, nx),
@@ -384,11 +443,12 @@
             held(YS, PLANE, 2, ZS, LANES),
             held(CHUNKS, YS, PLANE, 2, ZS, LANES),
             held(HALF, 4, ROWS, LANES),
-            held(CHUNKS, 2, 2, HALF, ROWS, LANES),
+            held(CHUNKS, 2, HALF, ROWS, LANES),
             held(CHUNKS, 2, HALF, ROWS, LANES),
             held(ROWS, ZS, LANES),
             held(CHUNKS, ROWS, ZS, LANES),
             held(2, ROWS, ZS, LANES),
+            held(CHUNKS, ROWS, ZS, LANES), held(HALF, 4, ROWS, LANES), held(ROWS, ZS, LANES),
             dma((CHUNKS,)), dma((CHUNKS,)),
             dma((CHUNKS, 2)), dma((CHUNKS,)),
             dma((CHUNKS, 2, 3)), dma((CHUNKS, 2)), dma((CHUNKS, 2)),
@@ -396,6 +456,7 @@
             dma((CHUNKS, 2)), dma((CHUNKS, 2)),
             dma((CHUNKS,)), dma((CHUNKS,)),
             dma((2,)), dma, dma((4,)), dma((2,)), dma((2,)), dma,
+            dma, dma((2,)), dma((2,)), dma((2,)),
         ],
         compiler_params=pltpu.CompilerParams(
             collective_id=0, has_side_effects=True, vmem_limit_bytes=62 * 2**20
@@ -438,7 +499,7 @@
 
 def per_device(scalar_field, x_operator, y_second, y_first, y_stretch, y_curve, z_operator):
     return copied(laplacian(
-        scalar_field, x_operator, y_second, y_first, y_stretch[None, :], y_curve[None, :], z_operator
+        scalar_field, x_operator, y_second, y_first, y_stretch, y_curve, z_operator
     ))
 
 

time: 242 us -> 234 us (0.967)
  Pallas kernels: 238 us -> 233 us
  local copies, waits for them, and re-layouts: 2.53 us -> 0 us
    pallas_call x1, Pallas kernels: 231 us -> 225 us  [laplacian(): pl.pallas_call(laplacian_kernel, name='laplacian', out_shape=(shape(ROWS,...]
    broadcast_in_dim x2 -> x0, local copies, waits for them, and re-layouts: 2.53 us -> none  [the longest x1 1.27 us: per_device(): y_stretch[None, :]]
where the time goes in v3:
time: 234 us; the launch traced here: 233 us
  Pallas kernels  233 us (100%)
    pallas_call x1, Pallas kernels, laplacian(): pl.pallas_call(laplacian_kernel, name='laplacian', out_shape=(shape(ROWS,...  225 us
    pallas_call x1, Pallas kernels, copied(): pl.pallas_call(copy_kernel, name='result', in_specs=[any_space], out_spec...  7.27 us

profile of v3, /device:TPU:0, one launch (start us, length us, event | category | flops | bytes accessed | tf_op | source)
XLA Modules:
  0.0 232.5 jit_solution(9406152529157787195)
XLA Ops:
  0.0 225.3 %laplacian.1 = (bf16[192,24,1024]{2,1,0:T(8,128)(2,1)}, bf16[4,192,24,128]{3,2,1,0:T(8,128)(2,1)}, bf16[4,12,16,2,24,128]{5,4,3,2,1,0:T(8,128)(2,1)}, bf16[4,2,1...) custom-call(bf16[192,24,1024]{2,1,0:T(8,128)(2,1)} %field.1, ...), custom_call_target="tpu_custom_call" | custom-call | flops 24199999488 | bytes 180000000 | tf_op jit(solution)/shard_map/laplacian/pallas_call | solution.py:422
  225.3 7.3 %result.1 = bf16[192,24,1024]{2,1,0:T(8,128)(2,1)} custom-call(bf16[192,24,1024]{2,1,0:T(8,128)(2,1)} %get-tuple-element.6.source), custom_call_target="tpu_custom_call" | custom-call | tf_op jit(solution)/shard_map/result/pallas_call | solution.py:486

commit v4 on v3

--- a/solution.py
+++ b/solution.py
@@ -26,9 +26,9 @@
     field, x_source, y_second, y_first, y_stretch, y_curve, z_source,
     total, traded, z_in, y_in, z_out, x_term,
     x_op, y_parts, y_op, z_raw, z_op, x_tile, x_result, x_got,
-    turn, staged, block, z_pencil, z_result, y_pencil, y_result, y_got, z_got, summed, final,
+    turn, staged, block, z_pencil, z_result, y_pencil, y_result, y_got, z_got, summed,
     back, y_last, z_last,
-    lo_s, lo_r, zi_s, zi_r, g_s, g_l, g_r, zo_s, zo_r, ys_s, ys_r, back_s, back_r, keep_l, load, ops_l, x_l, x_s,
+    lo_s, lo_r, zi_s, zi_r, g_s, g_l, g_r, zo_s, zo_r, ys_s, ys_r, back_s, back_r, load, ops_l, x_l, x_s,
     x_g, z_l, last_r, last_ys_s, last_ys_r,
 ):
     row, col = lax.axis_index("row"), lax.axis_index("col")
@@ -264,20 +264,6 @@
     def x_fetch(i, own):
         return pltpu.make_async_copy(x_term.at[(upper if own else 1 - upper) * CHUNKS + i], x_got, x_g)
 
-    order = [(0, False), (1, False), (0, True), (2, False), (1, True), (2, True), (3, False), (3, True)]
-
-    def keep_rows(i, own, first):
-        n, rows = order.index((i, own)) % 2, pl.ds(first, ROWS // 2)
-        return pltpu.make_async_copy(
-            final.at[n, rows], total.at[rows, :, lanes(mine if own else theirs, i)], keep_l.at[n]
-        )
-
-    def slot_for(i, own):
-        n = order.index((i, own))
-        if n >= 2:
-            drain(final.at[n % 2], keep_l.at[n % 2])
-        return n % 2
-
     def combine(i, own):
         part, half = (0, lo) if own else (1, other_lo)
         last = own and i == LAST
@@ -305,39 +291,33 @@
 
         if own:
             x_fetch(i, True).wait()
-            slot = slot_for(i, True)
+        elif i >= 2:
+            drain(summed.at[i % 2], back_s.at[i - 2])
         if last:
             drain(z_last, zo_r.at[i, half])
         else:
             z_fetch.wait()
-        for first in (0, ROWS // 2):
-            @pl.loop(0, ROWS // 32)
-            def _(j):
-                rows = pl.ds(first + j * 16, 16)
-                both = turn[pl.ds((first + j * 16) * ZS, 16 * ZS)].reshape(16, ZS, LANES) + z_term[rows].astype(F32)
-                if own:
-                    final[slot, rows] = (both + x_got[rows]).astype(BF16)
-                else:
-                    summed[i, rows] = both.astype(BF16)
-
+        @pl.loop(0, ROWS // 16)
+        def _(j):
+            rows = pl.ds(j * 16, 16)
+            both = turn[pl.ds(j * 16 * ZS, 16 * ZS)].reshape(16, ZS, LANES) + z_term[rows].astype(F32)
             if own:
-                keep_rows(i, True, first).start()
+                total[rows, :, lanes(mine, i)] = (both + x_got[rows]).astype(BF16)
+            else:
+                summed[i % 2, rows] = both.astype(BF16)
 
         if not own:
-            remote(summed.at[i], back.at[i], back_s.at[i], back_r.at[i], lo_peer).start()
+            remote(summed.at[i % 2], back.at[i], back_s.at[i], back_r.at[i], lo_peer).start()
 
     def finish(i):
         x_fetch(i, False).start()
         drain(back.at[i], back_r.at[i])
         x_fetch(i, False).wait()
-        slot = slot_for(i, False)
-        for first in (0, ROWS // 2):
-            @pl.loop(0, ROWS // 32)
-            def _(j):
-                rows = pl.ds(first + j * 16, 16)
-                final[slot, rows] = (back[i, rows].astype(F32) + x_got[rows]).astype(BF16)
-
-            keep_rows(i, False, first).start()
+
+        @pl.loop(0, ROWS // 16)
+        def _(j):
+            rows = pl.ds(j * 16, 16)
+            total[rows, :, lanes(theirs, i)] = (back[i, rows].astype(F32) + x_got[rows]).astype(BF16)
 
     def take(i):
         drain(traded.at[i], lo_r.at[i])
@@ -353,33 +333,35 @@
     for i in range(1, CHUNKS):
         send_y(i, True)
     loads[0].wait()
-    steps = ROWS // XS
-    do_x(0, steps // 2)
+    do_x(0, 8)
     take(0)
     make_y_op()
     make_z_op()
     do_y(0, False)
-    do_x(steps // 2, steps)
-    for slot in range(2):
-        x_store(slot, slot).wait()
+    do_x(8, 13)
     take(1)
     do_z(0)
     return_z(0, False)
     send_z(3, True)
     do_y(1, False)
+    do_x(13, 18)
     take(2)
     do_z(1)
     return_z(1, False)
     combine(0, False)
     do_y(2, False)
+    do_x(18, 21)
     take(3)
     do_z(2)
     return_z(2, False)
     combine(1, False)
+    do_x(21, 24)
     do_z(3)
     return_z(3, False)
     for i in range(CHUNKS):
         return_z(i, True)
+    for slot in range(2):
+        x_store(slot, slot).wait()
     do_y(3, False)
     finish(0)
     do_y(0, True)
@@ -407,9 +389,9 @@
             drain(z_out.at[i, half, pl.ds(0, (PLANE - 1) * YS)], zo_s.at[i, half])
         if i != LAST:
             drain(y_got.at[i, 0], ys_s.at[i, 0])
-        drain(summed.at[i], back_s.at[i])
+        if i >= 2:
+            drain(summed.at[i % 2], back_s.at[i])
     for n in range(2):
-        drain(final.at[n], keep_l.at[n])
         drain(y_got.at[LAST, 0, pl.ds(0, QUARTER)], last_ys_s.at[n])
 
 
@@ -423,7 +405,7 @@
         laplacian_kernel,
         name="laplacian",
         out_shape=(
-            shape(ROWS, ZS, nx),
+            held(ROWS, ZS, nx),
             shape(CHUNKS, ROWS, ZS, LANES),
             shape(CHUNKS, YS, PLANE, 2, ZS, LANES),
             shape(CHUNKS, 2, HALF, 4, ROWS, LANES),
@@ -431,7 +413,7 @@
             jax.ShapeDtypeStruct((2 * CHUNKS, ROWS, ZS, LANES), F32),
         ),
         in_specs=[any_space] * 4 + [vmem] * 2 + [any_space],
-        out_specs=(any_space,) * 6,
+        out_specs=(vmem,) + (any_space,) * 5,
         scratch_shapes=[
             held(nx, nx), held(2, NY, 2 * ROWS), held(2 * ROWS, NY), held(NZ, NZ), held(NZ, NZ),
             held(2, XS, ZS, nx),
@@ -446,7 +428,6 @@
             held(CHUNKS, 2, HALF, ROWS, LANES),
             held(CHUNKS, 2, HALF, ROWS, LANES),
             held(ROWS, ZS, LANES),
-            held(CHUNKS, ROWS, ZS, LANES),
             held(2, ROWS, ZS, LANES),
             held(CHUNKS, ROWS, ZS, LANES), held(HALF, 4, ROWS, LANES), held(ROWS, ZS, LANES),
             dma((CHUNKS,)), dma((CHUNKS,)),
@@ -455,50 +436,43 @@
             dma((CHUNKS, 2)), dma((CHUNKS, 2)),
             dma((CHUNKS, 2)), dma((CHUNKS, 2)),
             dma((CHUNKS,)), dma((CHUNKS,)),
-            dma((2,)), dma, dma((4,)), dma((2,)), dma((2,)), dma,
+            dma, dma((4,)), dma((2,)), dma((2,)), dma,
             dma, dma((2,)), dma((2,)), dma((2,)),
         ],
         compiler_params=pltpu.CompilerParams(
-            collective_id=0, has_side_effects=True, vmem_limit_bytes=62 * 2**20
+            collective_id=0, has_side_effects=True, vmem_limit_bytes=54 * 2**20
         ),
         cost_estimate=pl.CostEstimate(flops=24_200_000_000, bytes_accessed=180_000_000, transcendentals=0),
     )(*operands)[0]
 
 
-def copy_kernel(source, target, held, read, written):
-    parts = read.shape[0]
+def write_kernel(source, target, sems):
+    parts = sems.shape[0]
     rows = source.shape[0] // parts
-    piece = lambda n: pl.ds(n * rows, rows)
-    reads = [pltpu.make_async_copy(source.at[piece(n)], held.at[piece(n)], read.at[n]) for n in range(parts)]
-    writes = [pltpu.make_async_copy(held.at[piece(n)], target.at[piece(n)], written.at[n]) for n in range(parts)]
-    for copy in reads:
+    copies = [
+        pltpu.make_async_copy(source.at[pl.ds(n * rows, rows)], target.at[pl.ds(n * rows, rows)], sems.at[n])
+        for n in range(parts)
+    ]
+    for copy in copies:
         copy.start()
-    for n in range(parts):
-        reads[n].wait()
-        writes[n].start()
-    for copy in writes:
+    for copy in copies:
         copy.wait()
 
 
-def copied(array):
-    any_space = pl.BlockSpec(memory_space=pl.ANY)
-    parts = 12
+def written(array):
     return pl.pallas_call(
-        copy_kernel,
+        write_kernel,
         name="result",
-        in_specs=[any_space],
-        out_specs=any_space,
+        in_specs=[pl.BlockSpec(memory_space=pltpu.VMEM)],
+        out_specs=pl.BlockSpec(memory_space=pl.ANY),
         out_shape=jax.ShapeDtypeStruct(array.shape, array.dtype),
-        scratch_shapes=[
-            pltpu.VMEM(array.shape, array.dtype),
-            pltpu.SemaphoreType.DMA((parts,)), pltpu.SemaphoreType.DMA((parts,)),
-        ],
-        compiler_params=pltpu.CompilerParams(vmem_limit_bytes=60 * 2**20),
+        scratch_shapes=[pltpu.SemaphoreType.DMA((4,))],
+        compiler_params=pltpu.CompilerParams(vmem_limit_bytes=16 * 2**20),
     )(array)
 
 
 def per_device(scalar_field, x_operator, y_second, y_first, y_stretch, y_curve, z_operator):
-    return copied(laplacian(
+    return written(laplacian(
         scalar_field, x_operator, y_second, y_first, y_stretch, y_curve, z_operator
     ))
 

time: 234 us -> 230 us (0.983)
  Pallas kernels: 233 us -> 228 us
    pallas_call x2, Pallas kernels: 233 us -> 228 us  [the longest x1 224 us: laplacian(): pl.pallas_call(laplacian_kernel, name='laplacian', out_shape=(held(ROWS,...]
where the time goes in v4:
time: 230 us; the launch traced here: 228 us
  Pallas kernels  228 us (99%)
    pallas_call x1, Pallas kernels, laplacian(): pl.pallas_call(laplacian_kernel, name='laplacian', out_shape=(held(ROWS,...  224 us

profile of v4, /device:TPU:0, one launch (start us, length us, event | category | flops | bytes accessed | tf_op | source)
XLA Modules:
  0.0 228.1 jit_solution(5588134559269317227)
XLA Ops:
  0.0 224.4 %laplacian.1 = (bf16[192,24,1024]{2,1,0:T(8,128)(2,1)S(1)}, bf16[4,192,24,128]{3,2,1,0:T(8,128)(2,1)}, bf16[4,12,16,2,24,128]{5,4,3,2,1,0:T(8,128)(2,1)}, bf16[4...) custom-call(bf16[192,24,1024]{2,1,0:T(8,128)(2,1)} %field.1, ...), custom_call_target="tpu_custom_call" | custom-call | flops 24199999488 | bytes 180000000 | tf_op jit(solution)/shard_map/laplacian/pallas_call | solution.py:404
  224.4 3.7 %result.1 = bf16[192,24,1024]{2,1,0:T(8,128)(2,1)} custom-call(bf16[192,24,1024]{2,1,0:T(8,128)(2,1)S(1)} %get-tuple-element.6.source), custom_call_target="tpu_custom_call" | custom-call | tf_op jit(solution)/shard_map/result/pallas_call | solution.py:463

commit v5 on v4

--- a/solution.py
+++ b/solution.py
@@ -37,7 +37,7 @@
     pz, py = plane // 4, plane % 4
     upper = 1 - lax.rem(hi + lo, 2)
     mine, theirs = upper * (CHUNKS * LANES), (1 - upper) * (CHUNKS * LANES)
-    other_lo = 1 - lo
+    other_lo, other_core = 1 - lo, 1 - core
 
     lo_peer = (row, plane * 2 + other_lo)
     sibling = (hi * 2 + 1 - core, col)
@@ -78,6 +78,10 @@
     def x_load(j, slot):
         return pltpu.make_async_copy(field.at[pl.ds(j * XS, XS)], x_tile.at[slot], x_l.at[slot])
 
+    first_block = pltpu.make_async_copy(field.at[:, :, lanes(mine, 0)], block, load)
+    first_block.start()
+    x_load(0, 0).start()
+
     barrier = pltpu.get_barrier_semaphore()
     for peer in (lo_peer, sibling, far_same, far_cross):
         pl.semaphore_signal(barrier, inc=1, device_id=peer, device_id_type=MESH)
@@ -86,9 +90,17 @@
     def _(k):
         pl.semaphore_signal(barrier, inc=1, device_id=(row, plane_peer(k) * 2 + lo), device_id_type=MESH)
 
-    first_block = pltpu.make_async_copy(field.at[:, :, lanes(mine, 0)], block, load)
-    first_block.start()
-    x_load(0, 0).start()
+    def turn_block(i):
+        @pl.loop(0, ROWS // 16)
+        def _(j):
+            turn[pl.ds(j * 16 * ZS, 16 * ZS)] = block[pl.ds(j * 16, 16)].astype(F32).reshape(16 * ZS, LANES)
+
+        @pl.loop(0, ZS)
+        def _(z):
+            staged[i, z] = turn[pl.ds(z, ROWS, stride=ZS)].astype(BF16)
+
+    first_block.wait()
+    turn_block(0)
     pl.semaphore_wait(barrier, 4 + PLANE - 1)
 
     def part_of(i, own):
@@ -124,18 +136,11 @@
             drain(staged.at[i, pl.ds(0, HALF)], g_l.at[i, 0])
             for n in range(3):
                 drain(staged.at[i, pl.ds(0, HALF)], g_s.at[i, 0, n])
-        if own and i == 0:
-            first_block.wait()
-        else:
+        if not (own and i == 0):
             fetch(part_of(i, own), block)
 
-        @pl.loop(0, ROWS // 16)
-        def _(j):
-            turn[pl.ds(j * 16 * ZS, 16 * ZS)] = block[pl.ds(j * 16, 16)].astype(F32).reshape(16 * ZS, LANES)
-
-        @pl.loop(0, ZS)
-        def _(z):
-            staged[i, z] = turn[pl.ds(z, ROWS, stride=ZS)].astype(BF16)
+        if not (own and i == 0):
+            turn_block(i)
 
         keep, give = core * HALF, (1 - core) * HALF
         whole = pl.ds(0, HALF)
@@ -206,7 +211,7 @@
             z_op[here] = z_raw[:, here].astype(F32).T.astype(BF16)
 
     def x_store(j, slot):
-        return pltpu.make_async_copy(x_result.at[slot], x_term.at[:, pl.ds(j * XS, XS)], x_s.at[slot])
+        return pltpu.make_async_copy(x_result.at[slot], x_term.at[:, pl.ds(j * (XS * ZS), XS * ZS)], x_s.at[slot])
 
     def do_x(first, last):
         @pl.loop(first, last)
@@ -225,7 +230,7 @@
             flat = x_tile[slot].reshape(XS * ZS, 2 * CHUNKS * LANES)
             product = jnp.dot(flat, x_op[...], preferred_element_type=F32)
             for n in range(2 * CHUNKS):
-                x_result[slot, n] = product[:, n * LANES:(n + 1) * LANES].reshape(XS, ZS, LANES)
+                x_result[slot, n] = product[:, n * LANES:(n + 1) * LANES]
             x_store(j, slot).start()
 
     def y_products(i, held, first, last):
@@ -264,9 +269,11 @@
     def x_fetch(i, own):
         return pltpu.make_async_copy(x_term.at[(upper if own else 1 - upper) * CHUNKS + i], x_got, x_g)
 
+    def sixteen(ref, j):
+        return ref[pl.ds(j * (16 * ZS), 16 * ZS)].reshape(16, ZS, LANES)
+
     def combine(i, own):
         part, half = (0, lo) if own else (1, other_lo)
-        last = own and i == LAST
         if own:
             x_fetch(i, True).start()
 
@@ -274,16 +281,10 @@
         def _(z):
             turn[pl.ds(core * HALF + z, ROWS, stride=ZS)] = y_result[i, core, z].astype(F32)
 
-        if last:
-            z_term = z_last
-            for h in range(2):
-                drain(y_got.at[i, 0, pl.ds(0, QUARTER)], last_ys_r.at[h])
-        else:
-            z_term = z_got
-            drain(z_out.at[i, half], zo_r.at[i, half])
-            z_fetch = pltpu.make_async_copy(z_out.at[i, half], z_got, z_l)
-            z_fetch.start()
-            drain(y_got.at[i, part], ys_r.at[i, part])
+        drain(z_out.at[i, half], zo_r.at[i, half])
+        z_fetch = pltpu.make_async_copy(z_out.at[i, half], z_got, z_l)
+        z_fetch.start()
+        drain(y_got.at[i, part], ys_r.at[i, part])
 
         @pl.loop(0, HALF)
         def _(z):
@@ -293,31 +294,48 @@
             x_fetch(i, True).wait()
         elif i >= 2:
             drain(summed.at[i % 2], back_s.at[i - 2])
-        if last:
-            drain(z_last, zo_r.at[i, half])
-        else:
-            z_fetch.wait()
+        z_fetch.wait()
+
         @pl.loop(0, ROWS // 16)
         def _(j):
             rows = pl.ds(j * 16, 16)
-            both = turn[pl.ds(j * 16 * ZS, 16 * ZS)].reshape(16, ZS, LANES) + z_term[rows].astype(F32)
+            both = sixteen(turn, j) + z_got[rows].astype(F32)
             if own:
-                total[rows, :, lanes(mine, i)] = (both + x_got[rows]).astype(BF16)
+                total[rows, :, lanes(mine, i)] = (both + sixteen(x_got, j)).astype(BF16)
             else:
                 summed[i % 2, rows] = both.astype(BF16)
 
         if not own:
             remote(summed.at[i % 2], back.at[i], back_s.at[i], back_r.at[i], lo_peer).start()
 
+    def add_last(h, c):
+        @pl.loop(h * QUARTER, (h + 1) * QUARTER)
+        def _(z):
+            here = pl.ds(c * HALF + z, ROWS, stride=ZS)
+            term = y_result[LAST, core, z] if c is core else y_got[LAST, 0, z]
+            turn[here] = turn[here] + term.astype(F32)
+
+    def finish_last():
+        for h in range(2):
+            drain(y_got.at[LAST, 0, pl.ds(0, QUARTER)], last_ys_r.at[h])
+            add_last(h, other_core)
+        drain(z_last, zo_r.at[LAST, lo])
+
+        @pl.loop(0, ROWS // 16)
+        def _(j):
+            rows = pl.ds(j * 16, 16)
+            total[rows, :, lanes(mine, LAST)] = (sixteen(turn, j) + z_last[rows].astype(F32)).astype(BF16)
+
     def finish(i):
-        x_fetch(i, False).start()
+        if i != LAST:
+            x_fetch(i, False).start()
         drain(back.at[i], back_r.at[i])
         x_fetch(i, False).wait()
 
         @pl.loop(0, ROWS // 16)
         def _(j):
             rows = pl.ds(j * 16, 16)
-            total[rows, :, lanes(theirs, i)] = (back[i, rows].astype(F32) + x_got[rows]).astype(BF16)
+            total[rows, :, lanes(theirs, i)] = (back[i, rows].astype(F32) + sixteen(x_got, j)).astype(BF16)
 
     def take(i):
         drain(traded.at[i], lo_r.at[i])
@@ -326,8 +344,8 @@
 
     for i in range(CHUNKS):
         remote(field.at[:, :, lanes(theirs, i)], traded.at[i], lo_s.at[i], lo_r.at[i], lo_peer).start()
+    send_y(0, True)
     send_z(0, True)
-    send_y(0, True)
     send_z(1, True)
     send_z(2, True)
     for i in range(1, CHUNKS):
@@ -375,9 +393,15 @@
     combine(1, True)
     do_y_last(0)
     combine(2, True)
+    x_fetch(LAST, False).start()
+    x_last = pltpu.make_async_copy(x_term.at[upper * CHUNKS + LAST], turn, load)
+    x_last.start()
+    x_last.wait()
+    add_last(0, core)
     do_y_last(1)
-    finish(3)
-    combine(3, True)
+    finish(LAST)
+    add_last(1, core)
+    finish_last()
 
     for i in range(CHUNKS):
         drain(traded.at[i], lo_s.at[i])
@@ -410,15 +434,15 @@
             shape(CHUNKS, YS, PLANE, 2, ZS, LANES),
             shape(CHUNKS, 2, HALF, 4, ROWS, LANES),
             shape(CHUNKS, 2, ROWS, ZS, LANES),
-            jax.ShapeDtypeStruct((2 * CHUNKS, ROWS, ZS, LANES), F32),
+            jax.ShapeDtypeStruct((2 * CHUNKS, ROWS * ZS, LANES), F32),
         ),
         in_specs=[any_space] * 4 + [vmem] * 2 + [any_space],
         out_specs=(vmem,) + (any_space,) * 5,
         scratch_shapes=[
             held(nx, nx), held(2, NY, 2 * ROWS), held(2 * ROWS, NY), held(NZ, NZ), held(NZ, NZ),
             held(2, XS, ZS, nx),
-            pltpu.VMEM((2, 2 * CHUNKS, XS, ZS, LANES), F32),
-            pltpu.VMEM((ROWS, ZS, LANES), F32),
+            pltpu.VMEM((2, 2 * CHUNKS, XS * ZS, LANES), F32),
+            pltpu.VMEM((ROWS * ZS, LANES), F32),
             pltpu.VMEM((ROWS * ZS, LANES), F32),
             held(CHUNKS, ZS, ROWS, LANES),
             held(ROWS, ZS, LANES),

time: 230 us -> 223 us (0.970)
  Pallas kernels: 228 us -> 221 us
    pallas_call x1, Pallas kernels: 224 us -> 217 us  [laplacian(): pl.pallas_call(laplacian_kernel, name='laplacian', out_shape=(held(ROWS,...]
where the time goes in v5:
time: 223 us; the launch traced here: 221 us
  Pallas kernels  221 us (99%)
    pallas_call x1, Pallas kernels, laplacian(): pl.pallas_call(laplacian_kernel, name='laplacian', out_shape=(held(ROWS,...  217 us

profile of v5, /device:TPU:0, one launch (start us, length us, event | category | flops | bytes accessed | tf_op | source)
XLA Modules:
  0.0 220.9 jit_solution(14242887283573963684)
XLA Ops:
  0.0 217.2 %laplacian.1 = (bf16[192,24,1024]{2,1,0:T(8,128)(2,1)S(1)}, bf16[4,192,24,128]{3,2,1,0:T(8,128)(2,1)}, bf16[4,12,16,2,24,128]{5,4,3,2,1,0:T(8,128)(2,1)}, bf16[4...) custom-call(bf16[192,24,1024]{2,1,0:T(8,128)(2,1)} %field.1, ...), custom_call_target="tpu_custom_call" | custom-call | flops 24199999488 | bytes 180000000 | tf_op jit(solution)/shard_map/laplacian/pallas_call | solution.py:428
  217.2 3.7 %result.1 = bf16[192,24,1024]{2,1,0:T(8,128)(2,1)} custom-call(bf16[192,24,1024]{2,1,0:T(8,128)(2,1)S(1)} %get-tuple-element.6.source), custom_call_target="tpu_custom_call" | custom-call | tf_op jit(solution)/shard_map/result/pallas_call | solution.py:487

commit v6 on v5

--- a/solution.py
+++ b/solution.py
@@ -394,7 +394,7 @@
     do_y_last(0)
     combine(2, True)
     x_fetch(LAST, False).start()
-    x_last = pltpu.make_async_copy(x_term.at[upper * CHUNKS + LAST], turn, load)
+    x_last = pltpu.make_async_copy(x_term.at[upper * CHUNKS + LAST], turn.at[pl.ds(0, ROWS * ZS)], load)
     x_last.start()
     x_last.wait()
     add_last(0, core)
@@ -443,7 +443,7 @@
             held(2, XS, ZS, nx),
             pltpu.VMEM((2, 2 * CHUNKS, XS * ZS, LANES), F32),
             pltpu.VMEM((ROWS * ZS, LANES), F32),
-            pltpu.VMEM((ROWS * ZS, LANES), F32),
+            pltpu.VMEM((ROWS * ZS + ZS, LANES), F32),
             held(CHUNKS, ZS, ROWS, LANES),
             held(ROWS, ZS, LANES),
             held(YS, PLANE, 2, ZS, LANES),

time: 223 us -> 223 us (level)
  no operation moved by 1% of the time
where the time goes in v6:
time: 223 us; the launch traced here: 221 us
  Pallas kernels  221 us (99%)
    pallas_call x1, Pallas kernels, laplacian(): pl.pallas_call(laplacian_kernel, name='laplacian', out_shape=(held(ROWS,...  217 us

profile of v6, /device:TPU:0, one launch (start us, length us, event | category | flops | bytes accessed | tf_op | source)
XLA Modules:
  0.0 220.9 jit_solution(18001077705223020296)
XLA Ops:
  0.0 217.2 %laplacian.1 = (bf16[192,24,1024]{2,1,0:T(8,128)(2,1)S(1)}, bf16[4,192,24,128]{3,2,1,0:T(8,128)(2,1)}, bf16[4,12,16,2,24,128]{5,4,3,2,1,0:T(8,128)(2,1)}, bf16[4...) custom-call(bf16[192,24,1024]{2,1,0:T(8,128)(2,1)} %field.1, ...), custom_call_target="tpu_custom_call" | custom-call | flops 24199999488 | bytes 180000000 | tf_op jit(solution)/shard_map/laplacian/pallas_call | solution.py:428
  217.2 3.7 %result.1 = bf16[192,24,1024]{2,1,0:T(8,128)(2,1)} custom-call(bf16[192,24,1024]{2,1,0:T(8,128)(2,1)S(1)} %get-tuple-element.6.source), custom_call_target="tpu_custom_call" | custom-call | tf_op jit(solution)/shard_map/result/pallas_call | solution.py:487

commit v7 on v6

--- a/solution.py
+++ b/solution.py
@@ -15,7 +15,8 @@
 ZS = 24
 YS = ROWS // PLANE
 HALF = ZS // 2
-QUARTER = HALF // 2
+PIECES = 3
+PIECE = HALF // PIECES
 LAST = CHUNKS - 1
 XS = 8
 NY = 4 * ROWS
@@ -148,10 +149,10 @@
         far = y_target(i, z_half, not own, row)
         pieces = [(keep, far_same, 0, far), (give, far_cross, 1, far), (give, sibling, 2, near)]
         if i == LAST and not own:
-            for h in range(2):
+            for h in range(PIECES):
                 for z, peer, n, target in pieces[:2]:
                     remote(
-                        staged.at[i, pl.ds(z + h * QUARTER, QUARTER)], target.at[pl.ds(h * QUARTER, QUARTER)],
+                        staged.at[i, pl.ds(z + h * PIECE, PIECE)], target.at[pl.ds(h * PIECE, PIECE)],
                         g_s.at[i, part, n], last_r.at[h], peer,
                     ).start()
             pieces = pieces[2:]
@@ -259,9 +260,9 @@
         if h == 0:
             drain(y_got.at[LAST, 1], ys_s.at[LAST, 1])
             drain(y_last.at[:, 0], g_r.at[LAST, lo])
-        drain(y_last.at[pl.ds(0, QUARTER), pl.ds(0, 2)], last_r.at[h])
-        y_products(LAST, y_last, h * (QUARTER // 2), (h + 1) * (QUARTER // 2))
-        piece = pl.ds(h * QUARTER, QUARTER)
+        drain(y_last.at[pl.ds(0, PIECE), pl.ds(0, 2)], last_r.at[h])
+        y_products(LAST, y_last, h * (PIECE // 2), (h + 1) * (PIECE // 2))
+        piece = pl.ds(h * PIECE, PIECE)
         remote(
             y_result.at[LAST, 1 - core, piece], y_got.at[LAST, 0, piece], last_ys_s.at[h], last_ys_r.at[h], sibling
         ).start()
@@ -309,15 +310,15 @@
             remote(summed.at[i % 2], back.at[i], back_s.at[i], back_r.at[i], lo_peer).start()
 
     def add_last(h, c):
-        @pl.loop(h * QUARTER, (h + 1) * QUARTER)
+        @pl.loop(h * PIECE, (h + 1) * PIECE)
         def _(z):
             here = pl.ds(c * HALF + z, ROWS, stride=ZS)
             term = y_result[LAST, core, z] if c is core else y_got[LAST, 0, z]
             turn[here] = turn[here] + term.astype(F32)
 
     def finish_last():
-        for h in range(2):
-            drain(y_got.at[LAST, 0, pl.ds(0, QUARTER)], last_ys_r.at[h])
+        for h in range(PIECES):
+            drain(y_got.at[LAST, 0, pl.ds(0, PIECE)], last_ys_r.at[h])
             add_last(h, other_core)
         drain(z_last, zo_r.at[LAST, lo])
 
@@ -399,8 +400,10 @@
     x_last.wait()
     add_last(0, core)
     do_y_last(1)
+    add_last(1, core)
+    do_y_last(2)
     finish(LAST)
-    add_last(1, core)
+    add_last(2, core)
     finish_last()
 
     for i in range(CHUNKS):
@@ -415,8 +418,8 @@
             drain(y_got.at[i, 0], ys_s.at[i, 0])
         if i >= 2:
             drain(summed.at[i % 2], back_s.at[i])
-    for n in range(2):
-        drain(y_got.at[LAST, 0, pl.ds(0, QUARTER)], last_ys_s.at[n])
+    for n in range(PIECES):
+        drain(y_got.at[LAST, 0, pl.ds(0, PIECE)], last_ys_s.at[n])
 
 
 def laplacian(*operands):
@@ -461,7 +464,7 @@
             dma((CHUNKS, 2)), dma((CHUNKS, 2)),
             dma((CHUNKS,)), dma((CHUNKS,)),
             dma, dma((4,)), dma((2,)), dma((2,)), dma,
-            dma, dma((2,)), dma((2,)), dma((2,)),
+            dma, dma((PIECES,)), dma((PIECES,)), dma((PIECES,)),
         ],
         compiler_params=pltpu.CompilerParams(
             collective_id=0, has_side_effects=True, vmem_limit_bytes=54 * 2**20

time: 223 us -> 223 us (level)
  no operation moved by 1% of the time
where the time goes in v7:
time: 223 us; the launch traced here: 221 us
  Pallas kernels  221 us (99%)
    pallas_call x1, Pallas kernels, laplacian(): pl.pallas_call(laplacian_kernel, name='laplacian', out_shape=(held(ROWS,...  217 us

profile of v7, /device:TPU:0, one launch (start us, length us, event | category | flops | bytes accessed | tf_op | source)
XLA Modules:
  0.0 221.0 jit_solution(11559525799671200518)
XLA Ops:
  0.0 217.2 %laplacian.1 = (bf16[192,24,1024]{2,1,0:T(8,128)(2,1)S(1)}, bf16[4,192,24,128]{3,2,1,0:T(8,128)(2,1)}, bf16[4,12,16,2,24,128]{5,4,3,2,1,0:T(8,128)(2,1)}, bf16[4...) custom-call(bf16[192,24,1024]{2,1,0:T(8,128)(2,1)} %field.1, ...), custom_call_target="tpu_custom_call" | custom-call | flops 24199999488 | bytes 180000000 | tf_op jit(solution)/shard_map/laplacian/pallas_call | solution.py:431
  217.2 3.7 %result.1 = bf16[192,24,1024]{2,1,0:T(8,128)(2,1)} custom-call(bf16[192,24,1024]{2,1,0:T(8,128)(2,1)S(1)} %get-tuple-element.6.source), custom_call_target="tpu_custom_call" | custom-call | tf_op jit(solution)/shard_map/result/pallas_call | solution.py:490
